TPU v7x, 32 devices: a whole 2x2x4 slice. The times are simulated.
32 devices in a mesh: grp: 4 (over y, x), vid: 8 (over z, core).
Axes of the slice: x: 2, y: 2, z: 4, core: 2. Of those that a mesh axis runs over, the one named last changes fastest.
Arguments:
- frames: bfloat16 [32768, 1024], P(('grp', 'vid')), parts along dimension 0, may hold values from -240 to 240
- w_frame: bfloat16 [1024, 512], replicated, may hold values from -0.1875 to 0.1875
- step_emb: bfloat16 [4096, 512], P(('grp', 'vid')), parts along dimension 0, may hold values from -6 to 6
- targets: int32 [32768], P(('grp', 'vid')), parts along dimension 0, may hold values from 0 to 127
- tile_frame: int32 [32, 64], P(('grp', 'vid')), parts along dimension 0, may hold values from 0 to 7, as said below
- tile_step: int32 [32, 64], P(('grp', 'vid')), parts along dimension 0, may hold values from 0 to 7, as said below
- tile_count: int32 [32], P(('grp', 'vid')), parts along dimension 0, may hold values from 8 to 64, as said below
Outputs:
- row_loss: float32 [32768], P(('grp', 'vid')), parts along dimension 0
- frame_grad: bfloat16 [32768, 1024], P(('grp', 'vid')), parts along dimension 0
- step_grad: float32 [4096, 512], P(('grp', 'vid')), parts along dimension 0
There are 4 independent parts, one for each index of `grp`. A program takes and returns all parts, laid end to end along the dimension named above; an argument that names none is the same for every part. Nothing has to cross between parts.
Inputs may be any that keep to these rules, and one draw needn't show every extreme that they name: `tile_frame`: each run of 8 tiles of a list, starting at a multiple of 8, names every frame block once. `tile_step`: the (frame block, step block) pairs of one video's list are distinct; the first 8 tiles pair each frame block with the video's own step block. Only the first tile_count tiles of a list are valid; some video's list is full.
All inputs are finite; a program needn't handle non-finite values.
Results may differ from a plain program's by a relative error of at most 0.0086.
Values may be sent and summed in bfloat16 or wider, within the bound.
No kernel may reach another device: no remote copies, remote signals or barrier semaphores. Data moves between devices by JAX's collectives and lax.ppermute only.
A program may use at most 128 MiB of HBM per device.

v0:
```python
import math

import jax
import jax.numpy as jnp
from jax import lax
from jax.sharding import PartitionSpec as P


def shards(frames, w_frame, step_emb, targets, tile_frame, tile_step, tile_count):
    videos = lax.axis_size("vid")
    steps_own = step_emb.shape[0]
    width = step_emb.shape[1]
    frame_rows = frames.shape[0]
    temper = 1.0 / math.sqrt(width)
    blocks = frame_rows // 128
    embedded = jnp.dot(frames, w_frame, preferred_element_type=jnp.float32).astype(jnp.bfloat16)
    table = lax.all_gather(step_emb, "vid", axis=0, tiled=True)
    flat_table = table.reshape(videos, steps_own * width)
    frame_blocks = embedded.reshape(blocks, 128, width)
    rounds = tile_frame.shape[1] // blocks
    frame_tab = tile_frame.reshape(rounds, blocks)
    step_tab = tile_step.reshape(rounds, blocks)
    count = tile_count[0]
    block_ids = jnp.arange(blocks, dtype=jnp.int32)
    video_ids = jnp.arange(videos, dtype=jnp.int32)

    def round_scores(turn):
        frame_row = frame_tab[turn]
        step_row = step_tab[turn]
        slot_ok = (turn * blocks + block_ids < count).astype(jnp.int32)
        match = (frame_row[:, None] == block_ids[None, :]).astype(jnp.int32)
        step_for = jnp.sum(match * step_row[:, None], axis=0)
        valid = jnp.sum(match * slot_ok[:, None], axis=0) > 0
        picker = (step_for[:, None] == video_ids[None, :]).astype(jnp.bfloat16)
        cols = jnp.dot(picker, flat_table, preferred_element_type=jnp.float32).astype(jnp.bfloat16)
        cols = cols.reshape(blocks, steps_own, width)
        scores = (
            jnp.einsum("bre,bce->brc", frame_blocks, cols, preferred_element_type=jnp.float32)
            * temper
        )
        return (picker, valid, cols, scores)

    def forward_turn(carry, turn):
        best, total = carry
        picker, valid, cols, scores = round_scores(turn)
        tile_top = jnp.where(valid[:, None], jnp.max(scores, axis=2), -1e30)
        newest = jnp.maximum(best, tile_top)
        shifted = jnp.where(valid[:, None, None], scores - newest[:, :, None], -1e30)
        total = total * jnp.exp(best - newest) + jnp.sum(jnp.exp(shifted), axis=2)
        return ((newest, total), None)

    start_best = jnp.full((blocks, 128), -1e30, jnp.float32)
    start_total = jnp.zeros((blocks, 128), jnp.float32)
    (best, total), _ = lax.scan(
        forward_turn, (start_best, start_total), jnp.arange(rounds, dtype=jnp.int32)
    )
    lse = best + jnp.log(total)
    onehot = (targets[:, None] == jnp.arange(steps_own, dtype=jnp.int32)[None, :]).astype(
        jnp.bfloat16
    )
    chosen = jnp.dot(onehot, step_emb, preferred_element_type=jnp.float32)
    positive = jnp.sum(embedded.astype(jnp.float32) * chosen, axis=1) * temper
    row_loss = lse.reshape(-1) - positive

    def backward_turn(carry, turn):
        grad_frames, grad_steps = carry
        picker, valid, cols, scores = round_scores(turn)
        shifted = jnp.where(valid[:, None, None], scores - lse[:, :, None], -1e30)
        probs = jnp.exp(shifted).astype(jnp.bfloat16)
        toward_rows = (
            jnp.einsum("brc,bce->bre", probs, cols, preferred_element_type=jnp.float32) * temper
        )
        toward_cols = (
            jnp.einsum("brc,bre->bce", probs, frame_blocks, preferred_element_type=jnp.float32)
            * temper
        )
        added = lax.dot_general(
            picker.astype(jnp.float32),
            toward_cols.reshape(blocks, steps_own * width),
            (((0,), (0,)), ((), ())),
            precision=lax.Precision.HIGHEST,
            preferred_element_type=jnp.float32,
        )
        return ((grad_frames + toward_rows, grad_steps + added), None)

    start_frames = jnp.zeros((blocks, 128, width), jnp.float32)
    start_steps = jnp.zeros((videos, steps_own * width), jnp.float32)
    (grad_frames, grad_steps), _ = lax.scan(
        backward_turn, (start_frames, start_steps), jnp.arange(rounds, dtype=jnp.int32)
    )
    grad_rows = grad_frames.reshape(frame_rows, width) - chosen * temper
    frame_grad = lax.dot_general(
        grad_rows.astype(jnp.bfloat16),
        w_frame,
        (((1,), (1,)), ((), ())),
        preferred_element_type=jnp.float32,
    ).astype(jnp.bfloat16)
    flat_steps = grad_steps.reshape(videos * steps_own, width)
    returned = lax.psum_scatter(
        flat_steps.astype(jnp.bfloat16), "vid", scatter_dimension=0, tiled=True
    ).astype(jnp.float32)
    own_term = lax.dot_general(
        onehot, embedded, (((0,), (0,)), ((), ())), preferred_element_type=jnp.float32
    )
    step_grad = returned - own_term * temper
    return (row_loss, frame_grad, step_grad)


def solution(mesh):
    placed = (
        P(("grp", "vid"), None),
        P(),
        P(("grp", "vid"), None),
        P(("grp", "vid")),
        P(("grp", "vid"), None),
        P(("grp", "vid"), None),
        P(("grp", "vid")),
    )
    return jax.shard_map(
        shards,
        mesh=mesh,
        in_specs=placed,
        out_specs=(P(("grp", "vid")), P(("grp", "vid"), None), P(("grp", "vid"), None)),
        check_vma=False,
    )
```

profile of v0, /device:TPU:0, one launch (start us, length us, event | category | flops | bytes accessed | tf_op | source)
XLA Modules:
  0.0 227.2 jit_solution(5286313245962329016)
XLA Ops:
  8.5 1.3 reduce.6
  9.8 1.3 reduce.7
  11.3 2.8 %fusion.24 = f32[1024,512]{0,1:T(8,128)} fusion(bf16[128,512]{1,0:T(8,128)(2,1)} %param.13, s32[1024]{0:T(1024)} %param.14), kind=kOutput, calls=%fused_computation.52 | convolution fusion | flops 134348800 | bytes 2232320 | tf_op jit(solution)/shard_map/dot_general | solution.py:61
  14.2 3.0 %copy.20 = f32[1024,512]{1,0:T(8,128)} copy(f32[1024,512]{0,1:T(8,128)} %fusion.24) | data formatting | bytes 4194304 | tf_op jit(solution)/shard_map/dot_general | solution.py:61
  17.1 3.8 %multiply_reduce_fusion = (f32[1024]{0:T(1024)S(1)}, bf16[1024,512]{1,0:T(8,128)(2,1)}) fusion(f32[1024,512]{1,0:T(8,128)} %copy.20, bf16[1024,1024]{1,0:T(8,128)(2,1)S(1)} %copy-done, bf16[1024,512]{1,0:T(8,128)(2,1)S(1)} %copy-done.8), kind=kOutput, calls=%fused_computation.45 | convolution fusion | flops 1075837952 | bytes 6295552 | tf_op jit(solution)/shard_map/dot_general | solution.py:16
  21.0 13.5 %all-gather.2.cloned.1.call-done = bf16[1024,512]{1,0:T(8,128)(2,1)} async-done(((bf16[128,512]{1,0:T(8,128)(2,1)}), bf16[1024,512]{1,0:T(8,128)(2,1)}) %all-gather.2.cloned.1.call-update) | async-done | bytes 1048592 | tf_op jit(solution)/shard_map/all_gather | solution.py:17
  34.4 1.7 reshape.70
  36.2 43.0 %while.30 = (s32[]{:T(128)}, f32[8,128]{1,0:T(8,128)S(1)}, f32[8,128]{1,0:T(8,128)S(1)}, s32[8]{0:T(128)S(1)}, s32[8,8]{1,0:T(8,128)S(1)}, /*index=5*/s32[]{:T(1...) while((s32[]{:T(128)}, f32[8,128]{1,0:T(8,128)S(1)}, ...), condition=%wide.region_5.6_spmd.clone.clone, body=%wide.region_0.5_spmd.clone.clone.sunk | while | flops 143792544 | bytes 9491170 | solution.py:54
  79.8 103.0 %while.31 = (s32[]{:T(128)}, f32[8,128,512]{2,1,0:T(8,128)}, f32[8,65536]{1,0:T(8,128)}, s32[8]{0:T(128)S(1)}, s32[8,8]{1,0:T(8,128)S(1)}, /*index=5*/s32[]{:T(1...) while((s32[]{:T(128)}, f32[8,128,512]{2,1,0:T(8,128)}, ...), condition=%wide.region_10.11_spmd.clone.clone, body=%wide.region_7.10_spmd.clone.clone.sunk | while | flops 465568192 | bytes 61608848 | solution.py:88
  87.5 1.2 copy.40
  89.4 1.9 convolution_add_fusion.2
  91.4 1.3 copy-done.2
  102.3 1.9 convolution_add_fusion.2
  104.2 1.3 copy-done.2
  115.2 1.9 convolution_add_fusion.2
  117.1 1.3 copy-done.2
  128.0 1.9 convolution_add_fusion.2
  130.0 1.3 copy-done.2
  140.9 1.9 convolution_add_fusion.2
  142.9 1.3 copy-done.2
  153.8 1.9 convolution_add_fusion.2
  155.7 1.3 copy-done.2
  166.7 1.9 convolution_add_fusion.2
  168.6 1.3 copy-done.2
  179.6 1.9 convolution_add_fusion.2
  181.5 1.3 copy-done.2
  182.8 1.7 convert_element_type.62
  184.5 1.5 convert_element_type.63
  186.0 2.9 %copy.23 = f32[1024,512]{0,1:T(8,128)} copy(f32[1024,512]{1,0:T(8,128)} %bitcast.70) | data formatting | bytes 4194304 | tf_op jit(solution)/shard_map/reshape | solution.py:91
  188.9 5.2 %convolution_convert_fusion.2 = bf16[1024,1024]{1,0:T(8,128)(2,1)} fusion(bf16[1024,512]{1,0:T(8,128)(2,1)} %param.12, f32[1024,512]{0,1:T(8,128)} %copy.23, f32[1024,512]{0,1:T(8,128)} %fusion.24), kind=kOutput, calls=%fused_computation.46 | convolution fusion | flops 1076363264 | bytes 7340032 | tf_op jit(solution)/shard_map/dot_general | solution.py:92
  194.1 24.0 %reduce-scatter.2.cloned.1.call-done = bf16[128,512]{1,0:T(8,128)(2,1)} async-done(((bf16[1024,512]{1,0:T(8,128)(2,1)}), bf16[128,512]{1,0:T(8,128)(2,1)}) %reduce-scatter.2.cloned.1.call-update) | async-done | bytes 131088 | tf_op jit(solution)/shard_map/reduce_scatter | solution.py:99
  218.1 2.2 fusion.22
  (277 shorter events, 78.0 us)
Async XLA Ops:
  7.2 10.0 %copy-start = (bf16[1024,1024]{1,0:T(8,128)(2,1)S(1)}, bf16[1024,1024]{1,0:T(8,128)(2,1)}, u32[]{:S(2)}) copy-start(bf16[1024,1024]{1,0:T(8,128)(2,1)} %param.11) | copy-start | bytes 6291460
  7.2 27.3 %all-gather.2.cloned.1.call-start = ((), (), s32[]{:S(2)}) async-start(), calls=%async_computation.1 | async-start | bytes 1179648 | tf_op jit(solution)/shard_map/all_gather | solution.py:17
  7.9 210.2 %reduce-scatter.2.cloned.1.call-start = ((), (), s32[]{:S(2)}) async-start(), calls=%async_computation.2 | async-start | bytes 1179648 | tf_op jit(solution)/shard_map/reduce_scatter | solution.py:99
  14.2 3.0 %copy-start.8 = (bf16[1024,512]{1,0:T(8,128)(2,1)S(1)}, bf16[1024,512]{1,0:T(8,128)(2,1)}, u32[]{:S(2)}) copy-start(bf16[1024,512]{1,0:T(8,128)(2,1)} %param.12) | copy-start | bytes 3145732
  84.3 1.6 copy-start.3
  87.1 1.7 copy-start.4
  87.5 1.9 copy-start.1
  95.9 1.4 copy-start.6
  97.2 1.6 copy-start.3
  100.0 1.7 copy-start.4
  100.4 1.9 copy-start.1
  110.1 1.6 copy-start.3
  112.8 1.7 copy-start.4
  113.3 1.9 copy-start.1
  121.6 1.4 copy-start.6
  123.0 1.6 copy-start.3
  125.7 1.7 copy-start.4
  126.2 1.9 copy-start.1
  135.8 1.6 copy-start.3
  138.6 1.7 copy-start.4
  139.0 1.9 copy-start.1
  148.7 1.6 copy-start.3
  151.5 1.7 copy-start.4
  151.9 1.9 copy-start.1
  161.6 1.6 copy-start.3
  164.3 1.7 copy-start.4
  164.8 1.9 copy-start.1
  174.5 1.6 copy-start.3
  177.2 1.7 copy-start.4
  177.7 1.9 copy-start.1
  188.9 29.2 %copy-start.7 = (bf16[8,128,512]{2,1,0:T(8,128)(2,1)S(1)}, bf16[8,128,512]{2,1,0:T(8,128)(2,1)}, u32[]{:S(2)}) copy-start(bf16[8,128,512]{2,1,0:T(8,128)(2,1)} %get-tuple-element.562) | copy-start | bytes 3145732
  188.9 29.2 %copy-start.9 = (s32[1024]{0:T(1024)S(1)}, s32[1024]{0:T(1024)}, u32[]{:S(2)}) copy-start(s32[1024]{0:T(1024)} %param.14) | copy-start | bytes 12292
  (22 other events, 29.8 us)
Sparse Core Ops, SparseCore 0:
  9.6 24.7 all-gather.1
  186.1 31.9 reduce-scatter.1
where the time goes:
time: 229 us; the launch traced here: 227 us
  matrix products  58.6 us (26%)
  local copies, waits for them, and re-layouts  52.9 us (23%)
  loops' own time  43 us (19%)
  waiting for transfers between devices  38.2 us (17%)
  other arithmetic  20.4 us (9%)
  between operations  14.1 us (6%)
    while x112, local copies, waits for them, and re-layouts  33.6 us
    reduce_scatter x1, waiting for transfers between devices, shards(): lax.psum_scatter(flat_steps.astype(jnp.bfloat16), 'vid', scatter_dimensio...  24 us
    another operation x1, loops' own time, shards(): lax.scan(backward_turn, (start_frames, start_steps), jnp.arange(rounds, d...  21.6 us
    another operation x1, loops' own time, shards(): lax.scan(forward_turn, (start_best, start_total), jnp.arange(rounds, dtyp...  21.3 us
    dot_general x8, matrix products, backward_turn(): lax.dot_general(picker.astype(jnp.float32), toward_cols.reshape(blocks, s...  15.4 us
    all_gather x1, waiting for transfers between devices, shards(): table = lax.all_gather(step_emb, 'vid', axis=0, tiled=True)  13.5 us
    convert_element_type x16, other arithmetic, round_scores(): slot_ok = (turn * blocks + block_ids < count).astype(jnp.int32)  11.8 us
    dynamic_slice x16, local copies, waits for them, and re-layouts, shards(): lax.scan(forward_turn, (start_best, start_total), jnp.arange(rounds, dtyp...  9.35 us
  transfers between devices with their start and end apart: 2, of which 2 were waited for; matrix products, arithmetic and copies ran while one was open for 9% of the time, Pallas kernels for 0%

commit v1 on v0

v1 whole, which is shorter than its diff:
```python
import math

import jax
import jax.numpy as jnp
from jax import lax
from jax.experimental import pallas as pl
from jax.experimental.pallas import tpu as pltpu
from jax.sharding import PartitionSpec as P

F32 = jnp.float32
BF16 = jnp.bfloat16
HIDDEN = -1e30
EMBED_MIB = 52
NT = (((1,), (1,)), ((), ()))
TN = (((0,), (0,)), ((), ()))
VMEM = pl.BlockSpec(memory_space=pltpu.VMEM)
SMEM = pl.BlockSpec(memory_space=pltpu.SMEM)


def params(mib):
    return pltpu.CompilerParams(vmem_limit_bytes=mib * 2**20)


def cost(flops, nbytes, exps=0):
    return pl.CostEstimate(flops=flops, bytes_accessed=nbytes, transcendentals=exps)


def embed_kernel(x_ref, w_ref, e_ref):
    e_ref[...] = jnp.dot(x_ref[...], w_ref[...], preferred_element_type=F32).astype(BF16)


def embed(frames, w):
    rows, depth = frames.shape
    width = w.shape[1]
    tile = rows // 4
    return pl.pallas_call(
        embed_kernel,
        grid=(rows // tile,),
        in_specs=[
            pl.BlockSpec((tile, depth), lambda i: (i, 0)),
            pl.BlockSpec((depth, width), lambda i: (0, 0)),
        ],
        out_specs=pl.BlockSpec((tile, width), lambda i: (i, 0)),
        out_shape=jax.ShapeDtypeStruct((rows, width), BF16),
        cost_estimate=cost(2 * rows * depth * width, 2 * (rows * depth + depth * width + rows * width)),
        compiler_params=params(EMBED_MIB),
        name="embed",
    )(frames, w)


def sight(place, count, tf, ts, shape):
    videos, rows = shape
    chips = videos // 2
    slots = tf.shape[1]
    line = lax.broadcasted_iota(jnp.int32, (videos, slots), 0)
    slot = lax.broadcasted_iota(jnp.int32, (videos, slots), 1)
    back = (place >> 1) - (line >> 1)
    second = line & 1
    video = 2 * jnp.where(back < 0, back + chips, back)
    video = video + jnp.where((place & 1) == 0, second, 1 - second)
    left = jnp.where((ts == video) & (slot < count), 1.0, 0.0)
    block = lax.broadcasted_iota(jnp.int32, (rows, slots), 0) // 128
    right = jnp.where(tf == block, 1.0, 0.0)
    seen = lax.dot_general(left.astype(BF16), right.astype(BF16), NT, preferred_element_type=F32)
    return jnp.where(seen > 0.5, 0.0, HIDDEN)


def stack(refs):
    values = [ref[...] for ref in refs]
    return values[0] if len(values) == 1 else jnp.concatenate(values, axis=0)


def tiles(rows):
    return [slice(at, at + 256) for at in range(0, rows, 256)]


def score_kernel(k, parts, temper, *refs):
    e_ref = refs[0]
    blocks = refs[1 : 1 + parts]
    if k == 0:
        place_ref, count_ref, tf_ref, ts_ref, goal_ref = refs[1 + parts : 6 + parts]
        p_ref, top_ref, total_ref, pos_ref, bias_ref = refs[6 + parts :]
        bias_ref[...] = sight(place_ref[0], count_ref[0], tf_ref[...], ts_ref[...], bias_ref.shape)
    else:
        bias_ref, top_in, total_in, p_ref, top_ref, total_ref = refs[1 + parts :]
    chunk = stack(blocks)
    steps = chunk.shape[0]
    own = steps // 2
    for at in tiles(e_ref.shape[0]):
        s = lax.dot_general(chunk, e_ref[at, :], NT, preferred_element_type=F32) * temper
        bias = bias_ref[2 * k : 2 * k + 2, at]
        first, second = s[:own] + bias[0:1], s[own:] + bias[1:2]
        top = jnp.maximum(
            jnp.max(first, axis=0, keepdims=True), jnp.max(second, axis=0, keepdims=True)
        )
        if k == 0:
            hit = goal_ref[:, at] == lax.broadcasted_iota(jnp.int32, first.shape, 0)
            pos_ref[:, at] = jnp.sum(jnp.where(hit, s[:own], 0.0), axis=0, keepdims=True)
        else:
            top = jnp.maximum(top, top_in[:, at])
        first, second = jnp.exp(first - top), jnp.exp(second - top)
        p_ref[:own, at] = first
        p_ref[own:, at] = second
        total = jnp.sum(first, axis=0, keepdims=True) + jnp.sum(second, axis=0, keepdims=True)
        if k > 0:
            total = total + total_in[:, at] * jnp.exp(top_in[:, at] - top)
        top_ref[:, at] = top
        total_ref[:, at] = total


def score(k, videos, temper, e, chunk, *more):
    rows, width = e.shape
    steps = sum(part.shape[0] for part in chunk)
    line = jax.ShapeDtypeStruct((1, rows), F32)
    extra = [line, jax.ShapeDtypeStruct((videos, rows), F32)] if k == 0 else []
    specs = [SMEM, SMEM, VMEM, VMEM, VMEM] if k == 0 else [VMEM] * len(more)
    return pl.pallas_call(
        lambda *refs: score_kernel(k, len(chunk), temper, *refs),
        in_specs=[VMEM] * (1 + len(chunk)) + specs,
        out_specs=[VMEM] * (3 + len(extra)),
        out_shape=[jax.ShapeDtypeStruct((steps, rows), F32), line, line] + extra,
        cost_estimate=cost(
            2 * steps * rows * width, 2 * (rows + steps) * width + 4 * steps * rows, steps * rows
        ),
        compiler_params=params(24),
        name=f"score_{k}",
    )(e, *chunk, *more)


def share_kernel(k, *refs):
    p_ref, top_ref, last_ref, total_ref, e_ref = refs[:5]
    if k == 0:
        goal_ref, pos_ref, q_ref, mine_ref, other_ref, loss_ref = refs[5:]
        loss_ref[...] = last_ref[...] + jnp.log(total_ref[...]) - pos_ref[...]
    else:
        q_ref, mine_ref, other_ref = refs[5:]
    own = mine_ref.shape[0]
    scale = jnp.exp(top_ref[...] - last_ref[...]) / total_ref[...]
    out = None
    for at in tiles(e_ref.shape[0]):
        q = (p_ref[:, at] * scale[:, at]).astype(BF16)
        if k == 0:
            hit = goal_ref[:, at] == lax.broadcasted_iota(jnp.int32, q.shape, 0)
            q = (q.astype(F32) - jnp.where(hit, 1.0, 0.0)).astype(BF16)
        q_ref[:, at] = q
        part = jnp.dot(q, e_ref[at, :], preferred_element_type=F32)
        out = part if out is None else out + part
    mine_ref[...] = out[:own]
    other_ref[...] = out[own:].astype(BF16)


def share(k, p, top, last, total, e, *more):
    steps, rows = p.shape
    width = e.shape[1]
    own = steps // 2
    return pl.pallas_call(
        lambda *refs: share_kernel(k, *refs),
        in_specs=[VMEM] * (5 + len(more)),
        out_specs=[VMEM] * (4 if k == 0 else 3),
        out_shape=[
            jax.ShapeDtypeStruct((steps, rows), BF16),
            jax.ShapeDtypeStruct((own, width), F32),
            jax.ShapeDtypeStruct((own, width), BF16),
        ]
        + [jax.ShapeDtypeStruct((1, rows), F32)] * (k == 0),
        cost_estimate=cost(2 * steps * rows * width, 6 * steps * rows + 2 * rows * width),
        compiler_params=params(24),
        name=f"share_{k}",
    )(p, top, last, total, e, *more)


def back_kernel(sizes, temper, *refs):
    n = len(sizes)
    w_ref, out_ref = refs[0], refs[-1]
    rows = None
    at = 1 + n
    for k in range(n):
        chunk = stack(refs[at : at + sizes[k]])
        at += sizes[k]
        part = lax.dot_general(refs[1 + k][...], chunk, TN, preferred_element_type=F32)
        rows = part if rows is None else rows + part
    out_ref[...] = lax.dot_general(
        (rows * temper).astype(BF16), w_ref[...], NT, preferred_element_type=F32
    ).astype(BF16)


def back(w, qs, chunks, temper):
    n = len(qs)
    steps, rows = qs[0].shape
    depth, width = w.shape
    tile = rows // 4
    flat = [part for chunk in chunks for part in chunk]
    return pl.pallas_call(
        lambda *refs: back_kernel([len(chunk) for chunk in chunks], temper, *refs),
        grid=(rows // tile,),
        in_specs=[pl.BlockSpec((depth, width), lambda i: (0, 0))]
        + [pl.BlockSpec((steps, tile), lambda i: (0, i))] * n
        + [pl.BlockSpec(part.shape, lambda i: (0, 0)) for part in flat],
        out_specs=pl.BlockSpec((tile, depth), lambda i: (i, 0)),
        out_shape=jax.ShapeDtypeStruct((rows, depth), BF16),
        cost_estimate=cost(
            2 * rows * width * (n * steps + depth),
            2 * (n * steps * (rows + width) + depth * width + rows * depth),
        ),
        compiler_params=params(40),
        name="back",
    )(w, *qs, *flat)


def shards(frames, w_frame, step_emb, targets, tile_frame, tile_step, tile_count):
    videos = lax.axis_size("vid")
    chips = videos // 2
    far = chips // 2
    own, width = step_emb.shape
    half = own // 2
    temper = 1.0 / math.sqrt(width)
    place = lax.axis_index("vid").astype(jnp.int32)

    def along(x, k):
        pairs = [(i, (i // 2 + k) % chips * 2 + i % 2) for i in range(videos)]
        return lax.ppermute(x, "vid", pairs)

    def swap(x):
        return lax.ppermute(x, "vid", [(i, i ^ 1) for i in range(videos)])

    goals = targets.reshape(1, -1)
    e = embed(frames, w_frame)
    found = swap(step_emb)

    mine = {0: [step_emb]}
    right = left = step_emb
    for k in range(1, far):
        right, left = along(right, 1), along(left, -1)
        if k == 1:
            right, left, e = lax.optimization_barrier((right, left, e))
        mine[k], mine[chips - k] = [right], [left]
    mine[far] = [along(right[:half], 1), along(left[half:], -1)]

    order = [0] + [c for k in range(1, far) for c in (k, chips - k)] + [far]
    chunks, kept = {}, {}
    more = (place.reshape(1), tile_count, tile_frame, tile_step, goals)
    for k in order:
        if k == far and far > 1:
            (*mine[k], top) = lax.optimization_barrier((*mine[k], top))
        chunks[k] = mine[k] + ([found] if k == 0 else [swap(part) for part in mine[k]])
        p, top, total, *first = score(k, videos, temper, e, chunks[k], *more)
        kept[k] = (p, top)
        if k == 0:
            pos, bias = first
        more = (bias, top, total)
    last = top

    qs, whole = {}, {}
    for n, k in enumerate(reversed(order)):
        if n == 2:
            e, whole[far] = lax.optimization_barrier((e, whole[far]))
        if k == 0:
            e, qs[1] = lax.optimization_barrier((e, qs[1]))
        more = (goals, pos) if k == 0 else ()
        qs[k], part, other, *loss = share(k, *kept[k], last, total, e, *more)
        whole[k] = part + swap(other).astype(F32)
    right = along(whole[far][:half].astype(BF16), 1).astype(F32)
    left = along(whole[far][half:].astype(BF16), -1).astype(F32)
    for k in range(far - 1, 0, -1):
        up, down = whole[chips - k], whole[k]
        if k == far - 1:
            up = jnp.concatenate([up[:half] + right, up[half:]], axis=0)
            down = jnp.concatenate([down[:half], down[half:] + left], axis=0)
        else:
            up, down = up + right, down + left
        right = along(up.astype(BF16), 1).astype(F32)
        left = along(down.astype(BF16), -1).astype(F32)
    step_grad = (whole[0] + right + left) * temper
    frame_grad = back(
        w_frame, [qs[k] for k in order], [chunks[k] for k in order], temper
    )
    return (loss[0].reshape(-1), frame_grad, step_grad)


def solution(mesh):
    placed = (
        P(("grp", "vid"), None),
        P(),
        P(("grp", "vid"), None),
        P(("grp", "vid")),
        P(("grp", "vid"), None),
        P(("grp", "vid"), None),
        P(("grp", "vid")),
    )
    return jax.shard_map(
        shards,
        mesh=mesh,
        in_specs=placed,
        out_specs=(P(("grp", "vid")), P(("grp", "vid"), None), P(("grp", "vid"), None)),
        check_vma=False,
    )
```

time: 229 us -> 42 us (0.18)
  matrix products: 58.6 us -> 0 us
  local copies, waits for them, and re-layouts: 52.9 us -> 0.07 us
  loops' own time: 43 us -> 0 us
  waiting for transfers between devices: 38.2 us -> 9.91 us
  other arithmetic: 20.4 us -> 0.92 us
  starting transfers between devices: 0.08 us -> 16.4 us
  Pallas kernels: 0 us -> 13.1 us
  between operations: 14.1 us -> 1.5 us
    dot_general x60 -> x0, matrix products: 58.6 us -> none  [the longest x8 15.4 us: backward_turn(): lax.dot_general(picker.astype(jnp.float32), toward_cols.reshape(blocks, s...]
    another operation x2 -> x0, loops' own time: 43 us -> none  [the longest x1 21.6 us: shards(): lax.scan(backward_turn, (start_frames, start_steps), jnp.arange(rounds, d...]
    while x112 -> x0, local copies, waits for them, and re-layouts: 33.6 us -> none
    reduce_scatter x1 -> x0, waiting for transfers between devices: 24 us -> none  [shards(): lax.psum_scatter(flat_steps.astype(jnp.bfloat16), 'vid', scatter_dimensio...]
    ppermute x0 -> x17, starting transfers between devices: none -> 16.4 us  [the longest x8 14.2 us: along(): return lax.ppermute(x, 'vid', pairs)]
    convert_element_type x17 -> x0, other arithmetic: 13.5 us -> none  [the longest x16 11.8 us: round_scores(): slot_ok = (turn * blocks + block_ids < count).astype(jnp.int32)]
    all_gather x1 -> x0, waiting for transfers between devices: 13.5 us -> none  [shards(): table = lax.all_gather(step_emb, 'vid', axis=0, tiled=True)]
    pallas_call x0 -> x10, Pallas kernels: none -> 13.1 us  [the longest x1 4.46 us: back(): pl.pallas_call(lambda *refs: back_kernel([len(chunk) for chunk in chunks]...]
  transfers between devices with their start and end apart: 2 -> 17, of which waited for: 2 -> 10; matrix products, arithmetic and copies ran while one was open for 9% -> 0% of each run, Pallas kernels for 0% -> 29%
where the time goes in v1:
time: 42 us; the launch traced here: 41.9 us
  starting transfers between devices  16.4 us (39%)
  Pallas kernels  13.1 us (31%)
  waiting for transfers between devices  9.91 us (24%)
  between operations  1.5 us (4%)
  other arithmetic  0.92 us (2%)
    ppermute x8, starting transfers between devices, along(): return lax.ppermute(x, 'vid', pairs)  14.2 us
    ppermute x8, waiting for transfers between devices, along(): return lax.ppermute(x, 'vid', pairs)  7.87 us
    pallas_call x1, Pallas kernels, back(): pl.pallas_call(lambda *refs: back_kernel([len(chunk) for chunk in chunks]...  4.46 us
    pallas_call x1, Pallas kernels, embed(): pl.pallas_call(embed_kernel, grid=(rows // tile,), in_specs=[pl.BlockSpec...  3.82 us
    pallas_call x4, Pallas kernels, score(): pl.pallas_call(lambda *refs: score_kernel(k, len(chunk), temper, *refs),...  2.48 us
    pallas_call x4, Pallas kernels, share(): pl.pallas_call(lambda *refs: share_kernel(k, *refs), in_specs=[VMEM] * (5...  2.3 us
    ppermute x9, starting transfers between devices, swap(): return lax.ppermute(x, 'vid', [(i, i ^ 1) for i in range(videos)])  2.17 us
    ppermute x9, waiting for transfers between devices, swap(): return lax.ppermute(x, 'vid', [(i, i ^ 1) for i in range(videos)])  2.03 us
  transfers between devices with their start and end apart: 17, of which 10 were waited for; matrix products, arithmetic and copies ran while one was open for 0% of the time, Pallas kernels for 29%

profile of v1, /device:TPU:0, one launch (start us, length us, event | category | flops | bytes accessed | tf_op | source)
XLA Modules:
  0.0 41.9 jit_solution(15524408260549645990)
XLA Ops:
  0.7 5.1 %collective-permute-start.1 = (bf16[128,512]{1,0:T(8,128)(2,1)}, bf16[128,512]{1,0:T(8,128)(2,1)S(1)}, u32[]{:S(2)}, u32[]{:S(2)}) collective-permute-start(bf16[128,512]{1,0:T(8,128)(2,1)} %refs_5_.3), channel_id=1, source_target_pairs={{0,6},{1,7},{2,0},{3,1},{4,2},{5,3},{6,4},{7,5},{8,14},{9,15},{10,... | collective-permute-start | bytes 393224 | tf_op jit(solution)/shard_map/ppermute | solution.py:221
  5.8 3.8 %embed.1.refs_0_.refs_4_ = bf16[1024,512]{1,0:T(8,128)(2,1)S(1)} custom-call(bf16[1024,1024]{1,0:T(8,128)(2,1)} %x_ref.1, bf16[1024,512]{1,0:T(8,128)(2,1)} %refs_0_.1), custom_call_target="tpu_custom_call" | custom-call | flops 1073741824 | bytes 4194304 | tf_op jit(solution)/shard_map/embed/pallas_call | solution.py:36
  9.6 0.4 collective-permute-done.1.refs_1_.refs_9_
  10.0 2.8 %collective-permute-done.refs_1_.refs_7_ = bf16[128,512]{1,0:T(8,128)(2,1)S(1)} collective-permute-done((bf16[128,512]{1,0:T(8,128)(2,1)}, bf16[128,512]{1,0:T(8,128)(2,1)S(1)}, u32[]{:S(2)}, u32[]{:S(2)}) %collective-permute-start) | collective-permute-done | bytes 131104 | tf_op jit(solution)/shard_map/ppermute | solution.py:221
  12.8 0.5 %collective-permute-start.5 = (bf16[128,512]{1,0:T(8,128)(2,1)S(1)}, bf16[128,512]{1,0:T(8,128)(2,1)S(1)}, u32[]{:S(2)}, u32[]{:S(2)}) collective-permute-start(bf16[128,512]{1,0:T(8,128)(2,1)S(1)} %collective-permute-done.1.refs_1_.refs_9_), channel_id=1, source_target_pairs={{0,1},{1,0},{2,3},{3,2},{4,5},{5,4},{6,7},{7,6},{8,9},{9,8},{10,11... | collective-permute-start | bytes 393224 | tf_op jit(solution)/shard_map/ppermute | solution.py:224
  13.9 1.5 %collective-permute-start.4 = (bf16[64,512]{1,0:T(8,128)(2,1)S(1)}, bf16[64,512]{1,0:T(8,128)(2,1)S(1)}, u32[]{:S(2)}, u32[]{:S(2)}) collective-permute-start(bf16[64,512]{1,0:T(8,128)(2,1)S(1)} %slice.29), channel_id=1, source_target_pairs={{0,6},{1,7},{2,0},{3,1},{4,2},{5,3},{6,4},{7,5},{8,14},{9,15},{10,... | collective-permute-start | bytes 196616 | tf_op jit(solution)/shard_map/ppermute | solution.py:221
  15.5 0.6 %collective-permute-start.3 = (bf16[64,512]{1,0:T(8,128)(2,1)S(1)}, bf16[64,512]{1,0:T(8,128)(2,1)S(1)}, u32[]{:S(2)}, u32[]{:S(2)}) collective-permute-start(bf16[64,512]{1,0:T(8,128)(2,1)S(1)} %slice.28), channel_id=1, source_target_pairs={{0,2},{1,3},{2,4},{3,5},{4,6},{5,7},{6,0},{7,1},{8,10},{9,11},{10,... | collective-permute-start | bytes 196616 | tf_op jit(solution)/shard_map/ppermute | solution.py:221
  16.1 0.7 %score_0.1 = (f32[256,1024]{1,0:T(8,128)S(1)}, f32[1,1024]{1,0:T(1,128)S(1)}, f32[1,1024]{1,0:T(1,128)S(1)}, f32[1,1024]{1,0:T(1,128)S(1)}, f32[8,1024]{1,0:T(8,128)S(1)}) custom-call(bf16[1024,512]{1,0:T(8,128)(2,1)S(1)} %embed.1.refs_0_.refs_4_, bf16[128,512]{1,0:T(8,128)(2,1)S(1)} %copy-done.1, ...), custom_call_target="tpu_custom_call" | custom-call | flops 268435456 | bytes 2359296 | tf_op jit(solution)/shard_map/score_0/pallas_call | solution.py:117
  16.8 0.6 %score_1.1 = (f32[256,1024]{1,0:T(8,128)S(1)}, f32[1,1024]{1,0:T(1,128)S(1)}, f32[1,1024]{1,0:T(1,128)S(1)}) custom-call(bf16[1024,512]{1,0:T(8,128)(2,1)S(1)} %embed.1.refs_0_.refs_4_, bf16[128,512]{1,0:T(8,128)(2,1)S(1)} %collective-permute-done.refs_1_.refs_7_, bf16[128,512]{1,0:T(8,128)(2,1)S(1)} %collective-permute-done.6.refs_2_.refs_8_, ...), custom_call_target="tpu_custom_call" | custom-call | flops 268435456 | bytes 2359296 | tf_op jit(solution)/shard_map/score_1/pallas_call | solution.py:117
  17.4 0.6 %score_3.1 = (f32[256,1024]{1,0:T(8,128)S(1)}, f32[1,1024]{1,0:T(1,128)S(1)}, f32[1,1024]{1,0:T(1,128)S(1)}) custom-call(bf16[1024,512]{1,0:T(8,128)(2,1)S(1)} %embed.1.refs_0_.refs_4_, bf16[128,512]{1,0:T(8,128)(2,1)S(1)} %collective-permute-done.1.refs_1_.refs_9_, bf16[128,512]{1,0:T(8,128)(2,1)S(1)} %collective-permute-done.5.refs_2_.refs_10_, ...), custom_call_target="tpu_custom_call" | custom-call | flops 268435456 | bytes 2359296 | tf_op jit(solution)/shard_map/score_3/pallas_call | solution.py:117
  18.0 0.3 collective-permute-done.4.refs_2_.refs_12_
  18.3 3.3 %collective-permute-done.3.refs_1_.refs_11_ = bf16[64,512]{1,0:T(8,128)(2,1)S(1)} collective-permute-done((bf16[64,512]{1,0:T(8,128)(2,1)S(1)}, bf16[64,512]{1,0:T(8,128)(2,1)S(1)}, u32[]{:S(2)}, u32[]{:S(2)}) %collective-permute-start.3) | collective-permute-done | bytes 65568 | tf_op jit(solution)/shard_map/ppermute | solution.py:221
  21.5 0.5 %collective-permute-start.8 = (bf16[64,512]{1,0:T(8,128)(2,1)S(1)}, bf16[64,512]{1,0:T(8,128)(2,1)S(1)}, u32[]{:S(2)}, u32[]{:S(2)}) collective-permute-start(bf16[64,512]{1,0:T(8,128)(2,1)S(1)} %collective-permute-done.4.refs_2_.refs_12_), channel_id=1, source_target_pairs={{0,1},{1,0},{2,3},{3,2},{4,5},{5,4},{6,7},{7,6},{8,9},{9,8},{10,11... | collective-permute-start | bytes 196616 | tf_op jit(solution)/shard_map/ppermute | solution.py:224
  22.0 0.7 %collective-permute-done.7.refs_3_.refs_13_ = bf16[64,512]{1,0:T(8,128)(2,1)S(1)} collective-permute-done((bf16[64,512]{1,0:T(8,128)(2,1)S(1)}, bf16[64,512]{1,0:T(8,128)(2,1)S(1)}, u32[]{:S(2)}, u32[]{:S(2)}) %collective-permute-start.7) | collective-permute-done | bytes 65568 | tf_op jit(solution)/shard_map/ppermute | solution.py:224
  22.8 0.2 collective-permute-done.8.refs_4_.refs_14_
  22.9 0.6 %score_2.1 = (f32[256,1024]{1,0:T(8,128)S(1)}, f32[1,1024]{1,0:T(1,128)S(1)}, f32[1,1024]{1,0:T(1,128)S(1)}) custom-call(bf16[1024,512]{1,0:T(8,128)(2,1)S(1)} %embed.1.refs_0_.refs_4_, bf16[64,512]{1,0:T(8,128)(2,1)S(1)} %collective-permute-done.3.refs_1_.refs_11_, bf16[64,512]{1,0:T(8,128)(2,1)S(1)} %collective-permute-done.4.refs_2_.refs_12_, ...), custom_call_target="tpu_custom_call" | custom-call | flops 268435456 | bytes 2359296 | tf_op jit(solution)/shard_map/score_2/pallas_call | solution.py:117
  23.5 0.5 %share_2.1 = (bf16[256,1024]{1,0:T(8,128)(2,1)S(1)}, f32[128,512]{1,0:T(8,128)S(1)}, bf16[128,512]{1,0:T(8,128)(2,1)S(1)}) custom-call(f32[256,1024]{1,0:T(8,128)S(1)} %get-tuple-element.54.refs_0_, f32[1,1024]{1,0:T(1,128)S(1)} %get-tuple-element.52.refs_1_.refs_2_, f32[1,1024]{1,0:T(1,128)S(1)} %get-tuple-element.52.refs_1_.refs_2_, ...), custom_call_target="tpu_custom_call" | custom-call | flops 268435456 | bytes 2621440 | tf_op jit(solution)/shard_map/share_2/pallas_call | solution.py:156
  24.0 0.4 %collective-permute-start.9 = (bf16[128,512]{1,0:T(8,128)(2,1)S(1)}, bf16[128,512]{1,0:T(8,128)(2,1)S(1)}, u32[]{:S(2)}, u32[]{:S(2)}) collective-permute-start(bf16[128,512]{1,0:T(8,128)(2,1)S(1)} %get-tuple-element.56), channel_id=1, source_target_pairs={{0,1},{1,0},{2,3},{3,2},{4,5},{5,4},{6,7},{7,6},{8,9},{9,8},{10,11... | collective-permute-start | bytes 393224 | tf_op jit(solution)/shard_map/ppermute | solution.py:224
  24.4 0.5 %share_3.1 = (bf16[256,1024]{1,0:T(8,128)(2,1)S(1)}, f32[128,512]{1,0:T(8,128)S(1)}, bf16[128,512]{1,0:T(8,128)(2,1)S(1)}) custom-call(f32[256,1024]{1,0:T(8,128)S(1)} %get-tuple-element.65.refs_0_, f32[1,1024]{1,0:T(1,128)S(1)} %get-tuple-element.48.refs_6_.refs_1_, f32[1,1024]{1,0:T(1,128)S(1)} %get-tuple-element.52.refs_1_.refs_2_, ...), custom_call_target="tpu_custom_call" | custom-call | flops 268435456 | bytes 2621440 | tf_op jit(solution)/shard_map/share_3/pallas_call | solution.py:156
  24.9 0.2 collective-permute-start.11
  25.1 0.3 collective-permute-done.9
  25.5 0.1 collective-permute-start.12
  25.5 0.8 %collective-permute-done.11 = bf16[128,512]{1,0:T(8,128)(2,1)S(1)} collective-permute-done((bf16[128,512]{1,0:T(8,128)(2,1)S(1)}, bf16[128,512]{1,0:T(8,128)(2,1)S(1)}, u32[]{:S(2)}, u32[]{:S(2)}) %collective-permute-start.11) | collective-permute-done | bytes 131104 | tf_op jit(solution)/shard_map/ppermute | solution.py:224
  26.4 0.5 %share_1.1 = (bf16[256,1024]{1,0:T(8,128)(2,1)S(1)}, f32[128,512]{1,0:T(8,128)S(1)}, bf16[128,512]{1,0:T(8,128)(2,1)S(1)}) custom-call(f32[256,1024]{1,0:T(8,128)S(1)} %get-tuple-element.58.refs_0_, f32[1,1024]{1,0:T(1,128)S(1)} %get-tuple-element.46.refs_4_.refs_1_, f32[1,1024]{1,0:T(1,128)S(1)} %get-tuple-element.52.refs_1_.refs_2_, ...), custom_call_target="tpu_custom_call" | custom-call | flops 268435456 | bytes 2621440 | tf_op jit(solution)/shard_map/share_1/pallas_call | solution.py:156
  26.8 3.1 %collective-permute-start.15 = (bf16[64,512]{1,0:T(8,128)(2,1)S(1)}, bf16[64,512]{1,0:T(8,128)(2,1)S(1)}, u32[]{:S(2)}, u32[]{:S(2)}) collective-permute-start(bf16[64,512]{1,0:T(8,128)(2,1)S(1)} %get-tuple-element.76), channel_id=1, source_target_pairs={{0,6},{1,7},{2,0},{3,1},{4,2},{5,3},{6,4},{7,5},{8,14},{9,15},{10,... | collective-permute-start | bytes 196616 | tf_op jit(solution)/shard_map/ppermute | solution.py:221
  30.0 0.9 %share_0.1 = (bf16[256,1024]{1,0:T(8,128)(2,1)S(1)}, f32[128,512]{1,0:T(8,128)S(1)}, bf16[128,512]{1,0:T(8,128)(2,1)S(1)}, f32[1,1024]{1,0:T(1,128)}) custom-call(f32[256,1024]{1,0:T(8,128)S(1)} %get-tuple-element.40.refs_0_, f32[1,1024]{1,0:T(1,128)S(1)} %get-tuple-element.41.refs_4_.refs_1_, f32[1,1024]{1,0:T(1,128)S(1)} %get-tuple-element.52.refs_1_.refs_2_, ...), custom_call_target="tpu_custom_call" | custom-call | flops 268435456 | bytes 2621440 | tf_op jit(solution)/shard_map/share_0/pallas_call | solution.py:156
  30.9 0.5 %collective-permute-start.14 = (bf16[128,512]{1,0:T(8,128)(2,1)S(1)}, bf16[128,512]{1,0:T(8,128)(2,1)S(1)}, u32[]{:S(2)}, u32[]{:S(2)}) collective-permute-start(bf16[128,512]{1,0:T(8,128)(2,1)S(1)} %get-tuple-element.74), channel_id=1, source_target_pairs={{0,1},{1,0},{2,3},{3,2},{4,5},{5,4},{6,7},{7,6},{8,9},{9,8},{10,11... | collective-permute-start | bytes 393224 | tf_op jit(solution)/shard_map/ppermute | solution.py:224
  31.4 0.9 %collective-permute-done.12 = bf16[64,512]{1,0:T(8,128)(2,1)S(1)} collective-permute-done((bf16[64,512]{1,0:T(8,128)(2,1)S(1)}, bf16[64,512]{1,0:T(8,128)(2,1)S(1)}, u32[]{:S(2)}, u32[]{:S(2)}) %collective-permute-start.12) | collective-permute-done | bytes 65568 | tf_op jit(solution)/shard_map/ppermute | solution.py:221
  32.5 3.8 %collective-permute-start.16 = (bf16[128,512]{1,0:T(8,128)(2,1)S(1)}, bf16[128,512]{1,0:T(8,128)(2,1)S(1)}, u32[]{:S(2)}, u32[]{:S(2)}) collective-permute-start(bf16[128,512]{1,0:T(8,128)(2,1)S(1)} %pad_maximum_fusion.1), channel_id=1, source_target_pairs={{0,6},{1,7},{2,0},{3,1},{4,2},{5,3},{6,4},{7,5},{8,14},{9,15},{10,... | collective-permute-start | bytes 393224 | tf_op jit(solution)/shard_map/ppermute | solution.py:221
  36.3 4.5 %back.1 = bf16[1024,1024]{1,0:T(8,128)(2,1)} custom-call(bf16[1024,512]{1,0:T(8,128)(2,1)S(1)} %copy-done, bf16[256,1024]{1,0:T(8,128)(2,1)S(1)} %get-tuple-element.63.refs_1_, bf16[256,1024]{1,0:T(8,128)(2,1)S(1)} %get-tuple-element.64.refs_2_, bf16[256,1024]{1,0:T(8,128)(2,1)S(1)} %get-tuple-element.66.refs_3_, ...), custom_call_target="tpu_custom_call" | custom-call | flops 2147483648 | bytes 6291456 | tf_op jit(solution)/shard_map/back/pallas_call | solution.py:193
  40.8 0.3 collective-permute-done.16
  41.1 0.8 %add_multiply_fusion = f32[128,512]{1,0:T(8,128)} fusion(bf16[128,512]{1,0:T(8,128)(2,1)S(1)} %collective-permute-done.16, bf16[128,512]{1,0:T(8,128)(2,1)S(1)} %collective-permute-done.13, f32[128,512]{1,0:T(8,128)S(1)} %get-tuple-element.68, bf16[128,512]{1,0:T(8,128)(2,1)S(1)} %collective-permute-done.10), kind=kLoop, calls=%fused_computation | loop fusion | flops 458752 | bytes 917504 | tf_op jit(solution)/shard_map/mul | solution.py:273
  (35 shorter events, 0.4 us)
Async XLA Ops:
  0.6 15.4 %copy-start.1 = (bf16[128,512]{1,0:T(8,128)(2,1)S(1)}, bf16[128,512]{1,0:T(8,128)(2,1)}, u32[]{:S(2)}) copy-start(bf16[128,512]{1,0:T(8,128)(2,1)} %refs_5_.3) | copy-start | bytes 393220
  0.6 15.4 %copy-start.4 = (s32[1,64]{1,0:T(1,128)S(1)}, s32[1,64]{1,0:T(1,128)}, u32[]{:S(2)}) copy-start(s32[1,64]{1,0:T(1,128)} %refs_6_.1) | copy-start | bytes 772
  0.7 15.4 %copy-start.3 = (s32[1,64]{1,0:T(1,128)S(1)}, s32[1,64]{1,0:T(1,128)}, u32[]{:S(2)}) copy-start(s32[1,64]{1,0:T(1,128)} %refs_5_.2) | copy-start | bytes 772
  0.7 15.4 %copy-start.2 = (s32[1024]{0:T(1024)S(1)}, s32[1024]{0:T(1024)}, u32[]{:S(2)}) copy-start(s32[1024]{0:T(1024)} %param.10) | copy-start | bytes 12292
  0.7 9.3 %collective-permute-start.1 = (bf16[128,512]{1,0:T(8,128)(2,1)}, bf16[128,512]{1,0:T(8,128)(2,1)S(1)}, u32[]{:S(2)}, u32[]{:S(2)}) collective-permute-start(bf16[128,512]{1,0:T(8,128)(2,1)} %refs_5_.3), channel_id=1, source_target_pairs={{0,6},{1,7},{2,0},{3,1},{4,2},{5,3},{6,4},{7,5},{8,14},{9,15},{10,... | collective-permute-start | bytes 393224 | tf_op jit(solution)/shard_map/ppermute | solution.py:221
  5.8 7.0 %collective-permute-start = (bf16[128,512]{1,0:T(8,128)(2,1)}, bf16[128,512]{1,0:T(8,128)(2,1)S(1)}, u32[]{:S(2)}, u32[]{:S(2)}) collective-permute-start(bf16[128,512]{1,0:T(8,128)(2,1)} %refs_5_.3), channel_id=1, source_target_pairs={{0,2},{1,3},{2,4},{3,5},{4,6},{5,7},{6,0},{7,1},{8,10},{9,11},{10,... | collective-permute-start | bytes 393224 | tf_op jit(solution)/shard_map/ppermute | solution.py:221
  5.8 10.2 %collective-permute-start.2 = (bf16[128,512]{1,0:T(8,128)(2,1)}, bf16[128,512]{1,0:T(8,128)(2,1)S(1)}, u32[]{:S(2)}, u32[]{:S(2)}) collective-permute-start(bf16[128,512]{1,0:T(8,128)(2,1)} %refs_5_.3), channel_id=1, source_target_pairs={{0,1},{1,0},{2,3},{3,2},{4,5},{5,4},{6,7},{7,6},{8,9},{9,8},{10,11... | collective-permute-start | bytes 393224 | tf_op jit(solution)/shard_map/ppermute | solution.py:224
  12.8 4.0 %collective-permute-start.6 = (bf16[128,512]{1,0:T(8,128)(2,1)S(1)}, bf16[128,512]{1,0:T(8,128)(2,1)S(1)}, u32[]{:S(2)}, u32[]{:S(2)}) collective-permute-start(bf16[128,512]{1,0:T(8,128)(2,1)S(1)} %collective-permute-done.refs_1_.refs_7_), channel_id=1, source_target_pairs={{0,1},{1,0},{2,3},{3,2},{4,5},{5,4},{6,7},{7,6},{8,9},{9,8},{10,11... | collective-permute-start | bytes 393224 | tf_op jit(solution)/shard_map/ppermute | solution.py:224
  12.8 4.6 %collective-permute-start.5 = (bf16[128,512]{1,0:T(8,128)(2,1)S(1)}, bf16[128,512]{1,0:T(8,128)(2,1)S(1)}, u32[]{:S(2)}, u32[]{:S(2)}) collective-permute-start(bf16[128,512]{1,0:T(8,128)(2,1)S(1)} %collective-permute-done.1.refs_1_.refs_9_), channel_id=1, source_target_pairs={{0,1},{1,0},{2,3},{3,2},{4,5},{5,4},{6,7},{7,6},{8,9},{9,8},{10,11... | collective-permute-start | bytes 393224 | tf_op jit(solution)/shard_map/ppermute | solution.py:224
  13.9 4.3 %collective-permute-start.4 = (bf16[64,512]{1,0:T(8,128)(2,1)S(1)}, bf16[64,512]{1,0:T(8,128)(2,1)S(1)}, u32[]{:S(2)}, u32[]{:S(2)}) collective-permute-start(bf16[64,512]{1,0:T(8,128)(2,1)S(1)} %slice.29), channel_id=1, source_target_pairs={{0,6},{1,7},{2,0},{3,1},{4,2},{5,3},{6,4},{7,5},{8,14},{9,15},{10,... | collective-permute-start | bytes 196616 | tf_op jit(solution)/shard_map/ppermute | solution.py:221
  15.5 6.1 %collective-permute-start.3 = (bf16[64,512]{1,0:T(8,128)(2,1)S(1)}, bf16[64,512]{1,0:T(8,128)(2,1)S(1)}, u32[]{:S(2)}, u32[]{:S(2)}) collective-permute-start(bf16[64,512]{1,0:T(8,128)(2,1)S(1)} %slice.28), channel_id=1, source_target_pairs={{0,2},{1,3},{2,4},{3,5},{4,6},{5,7},{6,0},{7,1},{8,10},{9,11},{10,... | collective-permute-start | bytes 196616 | tf_op jit(solution)/shard_map/ppermute | solution.py:221
  21.5 1.3 %collective-permute-start.7 = (bf16[64,512]{1,0:T(8,128)(2,1)S(1)}, bf16[64,512]{1,0:T(8,128)(2,1)S(1)}, u32[]{:S(2)}, u32[]{:S(2)}) collective-permute-start(bf16[64,512]{1,0:T(8,128)(2,1)S(1)} %collective-permute-done.3.refs_1_.refs_11_), channel_id=1, source_target_pairs={{0,1},{1,0},{2,3},{3,2},{4,5},{5,4},{6,7},{7,6},{8,9},{9,8},{10,11... | collective-permute-start | bytes 196616 | tf_op jit(solution)/shard_map/ppermute | solution.py:224
  21.5 1.4 %collective-permute-start.8 = (bf16[64,512]{1,0:T(8,128)(2,1)S(1)}, bf16[64,512]{1,0:T(8,128)(2,1)S(1)}, u32[]{:S(2)}, u32[]{:S(2)}) collective-permute-start(bf16[64,512]{1,0:T(8,128)(2,1)S(1)} %collective-permute-done.4.refs_2_.refs_12_), channel_id=1, source_target_pairs={{0,1},{1,0},{2,3},{3,2},{4,5},{5,4},{6,7},{7,6},{8,9},{9,8},{10,11... | collective-permute-start | bytes 196616 | tf_op jit(solution)/shard_map/ppermute | solution.py:224
  24.0 1.4 %collective-permute-start.9 = (bf16[128,512]{1,0:T(8,128)(2,1)S(1)}, bf16[128,512]{1,0:T(8,128)(2,1)S(1)}, u32[]{:S(2)}, u32[]{:S(2)}) collective-permute-start(bf16[128,512]{1,0:T(8,128)(2,1)S(1)} %get-tuple-element.56), channel_id=1, source_target_pairs={{0,1},{1,0},{2,3},{3,2},{4,5},{5,4},{6,7},{7,6},{8,9},{9,8},{10,11... | collective-permute-start | bytes 393224 | tf_op jit(solution)/shard_map/ppermute | solution.py:224
  24.9 1.4 %collective-permute-start.11 = (bf16[128,512]{1,0:T(8,128)(2,1)S(1)}, bf16[128,512]{1,0:T(8,128)(2,1)S(1)}, u32[]{:S(2)}, u32[]{:S(2)}) collective-permute-start(bf16[128,512]{1,0:T(8,128)(2,1)S(1)} %get-tuple-element.71), channel_id=1, source_target_pairs={{0,1},{1,0},{2,3},{3,2},{4,5},{5,4},{6,7},{7,6},{8,9},{9,8},{10,11... | collective-permute-start | bytes 393224 | tf_op jit(solution)/shard_map/ppermute | solution.py:224
  25.5 6.8 %collective-permute-start.12 = (bf16[64,512]{1,0:T(8,128)(2,1)S(1)}, bf16[64,512]{1,0:T(8,128)(2,1)S(1)}, u32[]{:S(2)}, u32[]{:S(2)}) collective-permute-start(bf16[64,512]{1,0:T(8,128)(2,1)S(1)} %get-tuple-element.75), channel_id=1, source_target_pairs={{0,2},{1,3},{2,4},{3,5},{4,6},{5,7},{6,0},{7,1},{8,10},{9,11},{10,... | collective-permute-start | bytes 196616 | tf_op jit(solution)/shard_map/ppermute | solution.py:221
  26.8 9.5 %copy-start = (bf16[1024,512]{1,0:T(8,128)(2,1)S(1)}, bf16[1024,512]{1,0:T(8,128)(2,1)}, u32[]{:S(2)}) copy-start(bf16[1024,512]{1,0:T(8,128)(2,1)} %refs_0_.1) | copy-start | bytes 3145732
  26.8 5.6 %collective-permute-start.15 = (bf16[64,512]{1,0:T(8,128)(2,1)S(1)}, bf16[64,512]{1,0:T(8,128)(2,1)S(1)}, u32[]{:S(2)}, u32[]{:S(2)}) collective-permute-start(bf16[64,512]{1,0:T(8,128)(2,1)S(1)} %get-tuple-element.76), channel_id=1, source_target_pairs={{0,6},{1,7},{2,0},{3,1},{4,2},{5,3},{6,4},{7,5},{8,14},{9,15},{10,... | collective-permute-start | bytes 196616 | tf_op jit(solution)/shard_map/ppermute | solution.py:221
  30.9 9.9 %collective-permute-start.10 = (bf16[128,512]{1,0:T(8,128)(2,1)S(1)}, bf16[128,512]{1,0:T(8,128)(2,1)S(1)}, u32[]{:S(2)}, u32[]{:S(2)}) collective-permute-start(bf16[128,512]{1,0:T(8,128)(2,1)S(1)} %get-tuple-element.69), channel_id=1, source_target_pairs={{0,1},{1,0},{2,3},{3,2},{4,5},{5,4},{6,7},{7,6},{8,9},{9,8},{10,11... | collective-permute-start | bytes 393224 | tf_op jit(solution)/shard_map/ppermute | solution.py:224
  30.9 1.5 %collective-permute-start.14 = (bf16[128,512]{1,0:T(8,128)(2,1)S(1)}, bf16[128,512]{1,0:T(8,128)(2,1)S(1)}, u32[]{:S(2)}, u32[]{:S(2)}) collective-permute-start(bf16[128,512]{1,0:T(8,128)(2,1)S(1)} %get-tuple-element.74), channel_id=1, source_target_pairs={{0,1},{1,0},{2,3},{3,2},{4,5},{5,4},{6,7},{7,6},{8,9},{9,8},{10,11... | collective-permute-start | bytes 393224 | tf_op jit(solution)/shard_map/ppermute | solution.py:224
  32.3 8.5 %collective-permute-start.13 = (bf16[128,512]{1,0:T(8,128)(2,1)S(1)}, bf16[128,512]{1,0:T(8,128)(2,1)S(1)}, u32[]{:S(2)}, u32[]{:S(2)}) collective-permute-start(bf16[128,512]{1,0:T(8,128)(2,1)S(1)} %pad_maximum_fusion), channel_id=1, source_target_pairs={{0,2},{1,3},{2,4},{3,5},{4,6},{5,7},{6,0},{7,1},{8,10},{9,11},{10,... | collective-permute-start | bytes 393224 | tf_op jit(solution)/shard_map/ppermute | solution.py:221
  32.5 8.6 %collective-permute-start.16 = (bf16[128,512]{1,0:T(8,128)(2,1)S(1)}, bf16[128,512]{1,0:T(8,128)(2,1)S(1)}, u32[]{:S(2)}, u32[]{:S(2)}) collective-permute-start(bf16[128,512]{1,0:T(8,128)(2,1)S(1)} %pad_maximum_fusion.1), channel_id=1, source_target_pairs={{0,6},{1,7},{2,0},{3,1},{4,2},{5,3},{6,4},{7,5},{8,14},{9,15},{10,... | collective-permute-start | bytes 393224 | tf_op jit(solution)/shard_map/ppermute | solution.py:221

commit v2 on v0

v2 whole, which is shorter than its diff:
```python
import math

import jax
import jax.numpy as jnp
from jax import lax
from jax.experimental import pallas as pl
from jax.experimental.pallas import tpu as pltpu
from jax.sharding import PartitionSpec as P

F32 = jnp.float32
BF16 = jnp.bfloat16
HIDDEN = -1e30
EMBED_MIB = 52
TILES = 4
PIECES = 4
WIDE = 256
NT = (((1,), (1,)), ((), ()))
TN = (((0,), (0,)), ((), ()))
VMEM = pl.BlockSpec(memory_space=pltpu.VMEM)
SMEM = pl.BlockSpec(memory_space=pltpu.SMEM)
ANYWHERE = pl.BlockSpec(memory_space=pl.ANY)


def params(mib):
    return pltpu.CompilerParams(vmem_limit_bytes=mib * 2**20)


def cost(flops, nbytes, exps=0):
    return pl.CostEstimate(flops=flops, bytes_accessed=nbytes, transcendentals=exps)


def embed_kernel(x_hbm, w_hbm, e_ref, x_ref, w_ref, sem):
    tile = x_ref.shape[0] // TILES
    deep = w_ref.shape[0] // TILES
    reads = []
    for n in range(TILES):
        at = pl.ds(n * deep, deep)
        reads.append(pltpu.make_async_copy(w_hbm.at[at], w_ref.at[at], sem.at[n]))
    for n in range(TILES):
        at = pl.ds(n * tile, tile)
        reads.append(pltpu.make_async_copy(x_hbm.at[at], x_ref.at[at], sem.at[TILES + n]))
    for read in reads:
        read.start()
    for read in reads[:TILES]:
        read.wait()
    for n in range(TILES):
        reads[TILES + n].wait()
        at = slice(n * tile, (n + 1) * tile)
        e_ref[at, :] = jnp.dot(x_ref[at, :], w_ref[...], preferred_element_type=F32).astype(BF16)


def embed(frames, w):
    rows, depth = frames.shape
    width = w.shape[1]
    return pl.pallas_call(
        embed_kernel,
        in_specs=[ANYWHERE, ANYWHERE],
        out_specs=VMEM,
        out_shape=jax.ShapeDtypeStruct((rows, width), BF16),
        scratch_shapes=[
            pltpu.VMEM((rows, depth), BF16),
            pltpu.VMEM((depth, width), BF16),
            pltpu.SemaphoreType.DMA((2 * TILES,)),
        ],
        cost_estimate=cost(2 * rows * depth * width, 2 * (rows * depth + depth * width + rows * width)),
        compiler_params=params(EMBED_MIB),
        name="embed",
    )(frames, w)


def sight_kernel(place_ref, count_ref, tf_ref, ts_ref, keep_ref, give_ref):
    chips, rows = keep_ref.shape
    slots = tf_ref.shape[1]
    line = lax.broadcasted_iota(jnp.int32, (chips, slots), 0)
    slot = lax.broadcasted_iota(jnp.int32, (chips, slots), 1)
    block = lax.broadcasted_iota(jnp.int32, (rows, slots), 0) // 128
    right = jnp.where(tf_ref[...] == block, 1.0, 0.0).astype(BF16)
    for core, out_ref in enumerate((keep_ref, give_ref)):
        video = (2 * line + core) ^ place_ref[0]
        left = jnp.where((ts_ref[...] == video) & (slot < count_ref[0]), 1.0, 0.0).astype(BF16)
        seen = lax.dot_general(left, right, NT, preferred_element_type=F32)
        out_ref[...] = jnp.where(seen > 0.5, 0.0, HIDDEN)


def sight(place, count, tf, ts, chips, rows):
    return pl.pallas_call(
        sight_kernel,
        in_specs=[SMEM, SMEM, VMEM, VMEM],
        out_specs=[VMEM, VMEM],
        out_shape=[jax.ShapeDtypeStruct((chips, rows), F32)] * 2,
        compiler_params=params(24),
        name="sight",
    )(place, count, tf, ts)


def columns(rows):
    for half in range(2):
        for at in range(0, rows, WIDE):
            yield half, slice(at, at + WIDE), slice(half * rows + at, half * rows + at + WIDE)


def score_kernel(ks, temper, *refs):
    n = len(ks)
    es, biases = refs[:2], refs[2:4]
    blocks = refs[4 : 4 + n]
    refs = refs[4 + n :]
    if 0 in ks:
        goal_ref, st_in = refs[0], None
    else:
        st_in = refs[0]
    ps, tops = refs[1 : 1 + n], refs[1 + n : 1 + 2 * n]
    st_ref = refs[1 + 2 * n]
    rows = es[0].shape[0]
    for m, k in enumerate(ks):
        prior = st_in if m == 0 else st_ref
        for half, at, to in columns(rows):
            s = (
                lax.dot_general(blocks[m][...], es[half][at, :], NT, preferred_element_type=F32)
                * temper
            )
            if k == 0 and half == 0:
                hit = goal_ref[:, at] == lax.broadcasted_iota(jnp.int32, s.shape, 0)
                refs[2 + 2 * n][:, at] = jnp.sum(jnp.where(hit, s, 0.0), axis=0, keepdims=True)
            s = s + biases[half][k : k + 1, at]
            top = jnp.max(s, axis=0, keepdims=True)
            if prior is not None:
                top = jnp.maximum(top, prior[0:1, to])
            s = jnp.exp(s - top)
            ps[m][:, to] = s
            total = jnp.sum(s, axis=0, keepdims=True)
            if prior is not None:
                total = total + prior[1:2, to] * jnp.exp(prior[0:1, to] - top)
            tops[m][:, to] = top
            st_ref[0:1, to] = top
            st_ref[1:2, to] = total


def score(ks, temper, es, biases, blocks, last):
    rows, width = es[0].shape
    own = blocks[0].shape[0]
    shapes = [jax.ShapeDtypeStruct((own, 2 * rows), F32)] * len(ks)
    shapes += [jax.ShapeDtypeStruct((1, 2 * rows), F32)] * len(ks)
    shapes += [jax.ShapeDtypeStruct((2, 2 * rows), F32)]
    shapes += [jax.ShapeDtypeStruct((1, rows), F32)] * (0 in ks)
    made = pl.pallas_call(
        lambda *refs: score_kernel(ks, temper, *refs),
        in_specs=[VMEM] * (5 + len(ks)),
        out_specs=[VMEM] * len(shapes),
        out_shape=shapes,
        cost_estimate=cost(
            4 * len(ks) * own * rows * width, 4 * rows * width + 8 * len(ks) * own * rows
        ),
        compiler_params=params(24),
        name=f"score_{ks[-1]}",
    )(*es, *biases, *blocks, last)
    return made[: len(ks)], made[len(ks) : 2 * len(ks)], made[2 * len(ks) :]


def share_kernel(ks, *refs):
    st_ref, got_ref = refs[:2]
    es = refs[2:4]
    n = len(ks)
    ps, tops = refs[4 : 4 + n], refs[4 + n : 4 + 2 * n]
    refs = refs[4 + 2 * n :]
    if 0 in ks:
        goal_ref, pos_ref = refs[:2]
        refs = refs[2:]
    qs, outs = refs[:n], refs[n : 2 * n]
    rows = es[0].shape[0]
    for half in range(2):
        here = slice(half * rows, (half + 1) * rows)
        there = slice((1 - half) * rows, (2 - half) * rows)
        top, other = st_ref[0:1, here], got_ref[0:1, there]
        last = jnp.maximum(top, other)
        total = st_ref[1:2, here] * jnp.exp(top - last) + got_ref[1:2, there] * jnp.exp(other - last)
        if 0 in ks and half == 0:
            refs[2 * n][...] = last + jnp.log(total) - pos_ref[...]
        inverse = 1.0 / total
        for m, k in enumerate(ks):
            scale = jnp.exp(tops[m][:, here] - last) * inverse
            for at in range(0, rows, WIDE):
                to = slice(half * rows + at, half * rows + at + WIDE)
                q = (ps[m][:, to] * scale[:, at : at + WIDE]).astype(BF16)
                if k == 0 and half == 0:
                    hit = goal_ref[:, to] == lax.broadcasted_iota(jnp.int32, q.shape, 0)
                    q = (q.astype(F32) - jnp.where(hit, 1.0, 0.0)).astype(BF16)
                qs[m][:, to] = q
    for m in range(n):
        out = jnp.dot(qs[m][:, :rows], es[0][...], preferred_element_type=F32)
        out = out + jnp.dot(qs[m][:, rows:], es[1][...], preferred_element_type=F32)
        outs[m][...] = out.astype(outs[m].dtype)


def share(ks, kept, st, got, es, *more):
    own, rows2 = kept[ks[0]][0].shape
    width = es[0].shape[1]
    n = len(ks)
    shapes = [jax.ShapeDtypeStruct((own, rows2), BF16)] * n
    shapes += [jax.ShapeDtypeStruct((own, width), BF16 if k % 2 else F32) for k in ks]
    shapes += [jax.ShapeDtypeStruct((1, rows2 // 2), F32)] * (0 in ks)
    made = pl.pallas_call(
        lambda *refs: share_kernel(ks, *refs),
        in_specs=[VMEM] * (4 + 2 * n + len(more)),
        out_specs=[VMEM] * len(shapes),
        out_shape=shapes,
        cost_estimate=cost(2 * n * own * rows2 * width, n * 6 * own * rows2 + 2 * rows2 * width),
        compiler_params=params(40),
        name=f"share_{ks[0]}",
    )(st, got, *es, *[kept[k][0] for k in ks], *[kept[k][1] for k in ks], *more)
    return made[:n], made[n : 2 * n], made[2 * n :]


def part_rows(qs, table, at):
    q = jnp.concatenate([q_ref[:, at] for q_ref in qs], axis=0)
    return lax.dot_general(q, table, TN, preferred_element_type=F32)


def rows_kernel(n, first, *refs):
    table = jnp.concatenate([ref[...] for ref in refs[n : 2 * n]], axis=0)
    for turn, out_ref in enumerate(refs[2 * n :]):
        base = first + turn * out_ref.shape[0]
        for at in range(0, out_ref.shape[0], WIDE):
            part = part_rows(refs[:n], table, slice(base + at, base + at + WIDE))
            out_ref[at : at + WIDE, :] = part.astype(out_ref.dtype)


def rows_of(qs, blocks, theirs):
    n = len(qs)
    own, rows2 = qs[0].shape
    rows, width = rows2 // 2, blocks[0].shape[1]
    cut = PIECES if theirs else 1
    shape = jax.ShapeDtypeStruct((rows // cut, width), BF16 if theirs else F32)
    return pl.pallas_call(
        lambda *refs: rows_kernel(n, rows if theirs else 0, *refs),
        in_specs=[VMEM] * (2 * n),
        out_specs=[VMEM] * cut,
        out_shape=[shape] * cut,
        cost_estimate=cost(n * own * rows2 * width, 2 * n * own * (rows2 + width)),
        compiler_params=params(24),
        name="rows_theirs" if theirs else "rows_mine",
    )(*qs, *blocks)


def back_kernel(temper, mine_ref, w_ref, *refs):
    *gots, out_hbm, out_ref, sem = refs
    size = gots[0].shape[0]
    writes = []
    for turn, at in enumerate(range(0, out_ref.shape[0], WIDE)):
        cut = slice(at, at + WIDE)
        inner = slice(at % size, at % size + WIDE)
        g = (mine_ref[cut, :] + gots[at // size][inner, :].astype(F32)) * temper
        out_ref[cut, :] = lax.dot_general(
            g.astype(BF16), w_ref[...], NT, preferred_element_type=F32
        ).astype(BF16)
        cut = pl.ds(at, WIDE)
        writes.append(pltpu.make_async_copy(out_ref.at[cut], out_hbm.at[cut], sem.at[turn]))
        writes[-1].start()
    for write in writes:
        write.wait()


def back(mine, gots, w, temper):
    rows, width = mine.shape
    depth = w.shape[0]
    return pl.pallas_call(
        lambda *refs: back_kernel(temper, *refs),
        in_specs=[VMEM] * (2 + len(gots)),
        out_specs=ANYWHERE,
        out_shape=jax.ShapeDtypeStruct((rows, depth), BF16),
        scratch_shapes=[
            pltpu.VMEM((rows, depth), BF16),
            pltpu.SemaphoreType.DMA((rows // WIDE,)),
        ],
        cost_estimate=cost(2 * rows * width * depth, 2 * (depth * width + rows * depth)),
        compiler_params=params(40),
        name="back",
    )(mine, w, *gots)


def shards(frames, w_frame, step_emb, targets, tile_frame, tile_step, tile_count):
    videos = lax.axis_size("vid")
    chips = videos // 2
    rows = frames.shape[0]
    temper = 1.0 / math.sqrt(step_emb.shape[1])
    place = lax.axis_index("vid").astype(jnp.int32).reshape(1)
    goals = targets.reshape(1, -1)

    def trade(x, k):
        return lax.ppermute(x, "vid", [(i, i ^ k) for i in range(videos)])

    order, bit = [0], chips // 2
    while bit:
        order += [k ^ bit for k in order]
        bit //= 2
    e = embed(frames, w_frame)
    keep, lend = sight(place, tile_count, tile_frame, tile_step, chips, rows)
    biases = (keep, trade(lend, 1))
    mine, kept, st = {0: step_emb}, {}, goals
    for ks in [tuple(order[:2])] + [(k,) for k in order[2:]]:
        k = ks[-1]
        low = k & -k
        if 0 in ks:
            near = trade(step_emb, 2)
            come = trade(step_emb, 2 * low)
            mine[1], mine[k], e = lax.optimization_barrier((near, come, e))
            es = (e, trade(e, 1))
        elif k > 1:
            come = trade(mine[k ^ low], 2 * low)
            mine[k], gate = lax.optimization_barrier((come, st))
        ps, tops, (st, *pos) = score(ks, temper, es, biases, [mine[m] for m in ks], st)
        if pos:
            found = pos[0]
        for m, p, top in zip(ks, ps, tops):
            kept[m] = (p, top)
    got = trade(st, 1)

    qs, sums = {}, {}
    for ks in [(k,) for k in range(chips - 1, 2, -1)] + [(2, 1, 0)]:
        more = (goals, found) if 0 in ks else ()
        made, parts, loss = share(ks, kept, st, got, es, *more)
        qs.update(zip(ks, made))
        sums.update(zip(ks, parts))
        if 0 not in ks:
            e, qs[ks[0]] = lax.optimization_barrier((es[0], qs[ks[0]]))
            es = (e, es[1])
    parts = [qs[k] for k in order], [mine[k] for k in order]
    lent = [trade(piece, 1) for piece in rows_of(*parts, True)]
    (own_rows,) = rows_of(*parts, False)
    sums[1], own_rows = lax.optimization_barrier((sums[1], own_rows))
    frame_grad = back(own_rows, lent, w_frame, temper)
    bit = 1
    while bit < chips:
        for k in range(chips - bit, 0, -2 * bit):
            come = trade(sums[k].astype(BF16), 2 * bit)
            if 2 * bit == chips:
                come, frame_grad = lax.optimization_barrier((come, frame_grad))
            sums[k - bit] = sums[k - bit].astype(F32) + come.astype(F32)
        bit *= 2
    return (loss[0].reshape(-1), frame_grad, sums[0] * temper)


def solution(mesh):
    placed = (
        P(("grp", "vid"), None),
        P(),
        P(("grp", "vid"), None),
        P(("grp", "vid")),
        P(("grp", "vid"), None),
        P(("grp", "vid"), None),
        P(("grp", "vid")),
    )
    return jax.shard_map(
        shards,
        mesh=mesh,
        in_specs=placed,
        out_specs=(P(("grp", "vid")), P(("grp", "vid"), None), P(("grp", "vid"), None)),
        check_vma=False,
    )
```

time: 229 us -> 36.8 us (0.16)
  matrix products: 58.6 us -> 0 us
  local copies, waits for them, and re-layouts: 52.9 us -> 0.02 us
  loops' own time: 43 us -> 0 us
  waiting for transfers between devices: 38.2 us -> 8.36 us
  other arithmetic: 20.4 us -> 0.78 us
  starting transfers between devices: 0.08 us -> 13.7 us
  between operations: 14.1 us -> 1.43 us
  Pallas kernels: 0 us -> 12.4 us
    dot_general x60 -> x0, matrix products: 58.6 us -> none  [the longest x8 15.4 us: backward_turn(): lax.dot_general(picker.astype(jnp.float32), toward_cols.reshape(blocks, s...]
    another operation x2 -> x0, loops' own time: 43 us -> none  [the longest x1 21.6 us: shards(): lax.scan(backward_turn, (start_frames, start_steps), jnp.arange(rounds, d...]
    while x112 -> x0, local copies, waits for them, and re-layouts: 33.6 us -> none
    reduce_scatter x1 -> x0, waiting for transfers between devices: 24 us -> none  [shards(): lax.psum_scatter(flat_steps.astype(jnp.bfloat16), 'vid', scatter_dimensio...]
    ppermute x0 -> x13, starting transfers between devices: none -> 13.7 us  [trade(): return lax.ppermute(x, 'vid', [(i, i ^ k) for i in range(videos)])]
    convert_element_type x17 -> x1, other arithmetic: 13.5 us -> 0.03 us  [shards(): come = trade(sums[k].astype(BF16), 2 * bit)]
    all_gather x1 -> x0, waiting for transfers between devices: 13.5 us -> none  [shards(): table = lax.all_gather(step_emb, 'vid', axis=0, tiled=True)]
    pallas_call x0 -> x10, Pallas kernels: none -> 12.4 us  [the longest x3 3.4 us: score(): pl.pallas_call(lambda *refs: score_kernel(ks, temper, *refs), in_specs=[V...]
  transfers between devices with their start and end apart: 2 -> 13, of which waited for: 2 -> 7; matrix products, arithmetic and copies ran while one was open for 9% -> 0% of each run, Pallas kernels for 0% -> 30%
where the time goes in v2:
time: 36.8 us; the launch traced here: 36.6 us
  starting transfers between devices  13.7 us (37%)
  Pallas kernels  12.4 us (34%)
  waiting for transfers between devices  8.36 us (23%)
  between operations  1.43 us (4%)
  other arithmetic  0.78 us (2%)
    ppermute x13, starting transfers between devices, trade(): return lax.ppermute(x, 'vid', [(i, i ^ k) for i in range(videos)])  13.7 us
    ppermute x13, waiting for transfers between devices, trade(): return lax.ppermute(x, 'vid', [(i, i ^ k) for i in range(videos)])  8.36 us
    pallas_call x3, Pallas kernels, score(): pl.pallas_call(lambda *refs: score_kernel(ks, temper, *refs), in_specs=[V...  3.4 us
    pallas_call x1, Pallas kernels, embed(): pl.pallas_call(embed_kernel, in_specs=[ANYWHERE, ANYWHERE], out_specs=VME...  3.18 us
    pallas_call x1, Pallas kernels, back(): pl.pallas_call(lambda *refs: back_kernel(temper, *refs), in_specs=[VMEM]...  2.13 us
    pallas_call x2, Pallas kernels, share(): pl.pallas_call(lambda *refs: share_kernel(ks, *refs), in_specs=[VMEM] * (...  1.91 us
    pallas_call x2, Pallas kernels, rows_of(): pl.pallas_call(lambda *refs: rows_kernel(n, rows if theirs else 0, *refs)...  1.49 us
    mul x1, other arithmetic, shards(): return (loss[0].reshape(-1), frame_grad, sums[0] * temper)  0.75 us
  transfers between devices with their start and end apart: 13, of which 7 were waited for; matrix products, arithmetic and copies ran while one was open for 0% of the time, Pallas kernels for 30%

profile of v2, /device:TPU:0, one launch (start us, length us, event | category | flops | bytes accessed | tf_op | source)
XLA Modules:
  0.0 36.6 jit_solution(433847153297476212)
XLA Ops:
  0.7 4.1 %collective-permute-start.1 = (bf16[128,512]{1,0:T(8,128)(2,1)}, bf16[128,512]{1,0:T(8,128)(2,1)S(1)}, u32[]{:S(2)}, u32[]{:S(2)}) collective-permute-start(bf16[128,512]{1,0:T(8,128)(2,1)} %refs_4_.5), channel_id=1, source_target_pairs={{0,4},{1,5},{2,6},{3,7},{4,0},{5,1},{6,2},{7,3},{8,12},{9,13},{10,... | collective-permute-start | bytes 393224 | tf_op jit(solution)/shard_map/ppermute | solution.py:289
  4.8 1.6 %collective-permute-start = (bf16[128,512]{1,0:T(8,128)(2,1)}, bf16[128,512]{1,0:T(8,128)(2,1)S(1)}, u32[]{:S(2)}, u32[]{:S(2)}) collective-permute-start(bf16[128,512]{1,0:T(8,128)(2,1)} %refs_4_.5), channel_id=1, source_target_pairs={{0,2},{1,3},{2,0},{3,1},{4,6},{5,7},{6,4},{7,5},{8,10},{9,11},{10,... | collective-permute-start | bytes 393224 | tf_op jit(solution)/shard_map/ppermute | solution.py:289
  6.3 3.2 %embed.1.refs_0_.refs_2_ = bf16[1024,512]{1,0:T(8,128)(2,1)S(1)} custom-call(bf16[1024,1024]{1,0:T(8,128)(2,1)} %x_hbm.1, bf16[1024,512]{1,0:T(8,128)(2,1)} %refs_1_.1), custom_call_target="tpu_custom_call" | custom-call | flops 1073741824 | bytes 4194304 | tf_op jit(solution)/shard_map/embed/pallas_call | solution.py:55
  9.5 1.9 %collective-permute-done.1.refs_5_ = bf16[128,512]{1,0:T(8,128)(2,1)S(1)} collective-permute-done((bf16[128,512]{1,0:T(8,128)(2,1)}, bf16[128,512]{1,0:T(8,128)(2,1)S(1)}, u32[]{:S(2)}, u32[]{:S(2)}) %collective-permute-start.1) | collective-permute-done | bytes 131104 | tf_op jit(solution)/shard_map/ppermute | solution.py:289
  11.4 0.2 collective-permute-done.refs_4_.refs_6_
  11.6 0.0 collective-permute-start.2
  11.6 1.4 %collective-permute-start.4 = (bf16[128,512]{1,0:T(8,128)(2,1)S(1)}, bf16[128,512]{1,0:T(8,128)(2,1)S(1)}, u32[]{:S(2)}, u32[]{:S(2)}) collective-permute-start(bf16[128,512]{1,0:T(8,128)(2,1)S(1)} %collective-permute-done.1.refs_5_), channel_id=1, source_target_pairs={{0,2},{1,3},{2,0},{3,1},{4,6},{5,7},{6,4},{7,5},{8,10},{9,11},{10,... | collective-permute-start | bytes 393224 | tf_op jit(solution)/shard_map/ppermute | solution.py:289
  13.7 0.3 sight.1
  14.0 0.3 collective-permute-start.3
  14.3 1.0 %collective-permute-done.3.refs_3_ = f32[4,1024]{1,0:T(4,128)S(1)} collective-permute-done((f32[4,1024]{1,0:T(4,128)S(1)}, f32[4,1024]{1,0:T(4,128)S(1)}, u32[]{:S(2)}, u32[]{:S(2)}) %collective-permute-start.3) | collective-permute-done | bytes 16416 | tf_op jit(solution)/shard_map/ppermute | solution.py:289
  15.2 1.6 %score_2.1 = (f32[128,2048]{1,0:T(8,128)S(1)}, f32[128,2048]{1,0:T(8,128)S(1)}, f32[1,2048]{1,0:T(1,128)S(1)}, f32[1,2048]{1,0:T(1,128)S(1)}, f32[2,2048]{1,0:T(2,128)S(1)}, /*index=5*/f32[1,1024]{1,0:T(1,128)S(1)}) custom-call(bf16[1024,512]{1,0:T(8,128)(2,1)S(1)} %embed.1.refs_0_.refs_2_, bf16[1024,512]{1,0:T(8,128)(2,1)S(1)} %collective-permute-done.2.refs_1_.refs_3_, ...), custom_call_target="tpu_custom_call" | custom-call | flops 536870912 | bytes 4194304 | tf_op jit(solution)/shard_map/score_2/pallas_call | solution.py:145
  16.8 0.9 %score_1.1 = (f32[128,2048]{1,0:T(8,128)S(1)}, f32[1,2048]{1,0:T(1,128)S(1)}, f32[2,2048]{1,0:T(2,128)S(1)}) custom-call(bf16[1024,512]{1,0:T(8,128)(2,1)S(1)} %embed.1.refs_0_.refs_2_, bf16[1024,512]{1,0:T(8,128)(2,1)S(1)} %collective-permute-done.2.refs_1_.refs_3_, f32[4,1024]{1,0:T(4,128)S(1)} %get-tuple-element.41.refs_2_, ...), custom_call_target="tpu_custom_call" | custom-call | flops 268435456 | bytes 3145728 | tf_op jit(solution)/shard_map/score_1/pallas_call | solution.py:145
  17.7 0.9 %score_3.1 = (f32[128,2048]{1,0:T(8,128)S(1)}, f32[1,2048]{1,0:T(1,128)S(1)}, f32[2,2048]{1,0:T(2,128)S(1)}) custom-call(bf16[1024,512]{1,0:T(8,128)(2,1)S(1)} %embed.1.refs_0_.refs_2_, bf16[1024,512]{1,0:T(8,128)(2,1)S(1)} %collective-permute-done.2.refs_1_.refs_3_, f32[4,1024]{1,0:T(4,128)S(1)} %get-tuple-element.41.refs_2_, ...), custom_call_target="tpu_custom_call" | custom-call | flops 268435456 | bytes 3145728 | tf_op jit(solution)/shard_map/score_3/pallas_call | solution.py:145
  18.6 0.3 collective-permute-start.5
  18.9 1.0 %collective-permute-done.5.refs_1_ = f32[2,2048]{1,0:T(2,128)S(1)} collective-permute-done((f32[2,2048]{1,0:T(2,128)S(1)}, f32[2,2048]{1,0:T(2,128)S(1)}, u32[]{:S(2)}, u32[]{:S(2)}) %collective-permute-start.5) | collective-permute-done | bytes 16416 | tf_op jit(solution)/shard_map/ppermute | solution.py:289
  19.9 0.4 %share_3.1 = (bf16[128,2048]{1,0:T(8,128)(2,1)S(1)}, bf16[128,512]{1,0:T(8,128)(2,1)S(1)}) custom-call(f32[2,2048]{1,0:T(2,128)S(1)} %get-tuple-element.48.refs_0_, f32[2,2048]{1,0:T(2,128)S(1)} %collective-permute-done.5.refs_1_, bf16[1024,512]{1,0:T(8,128)(2,1)S(1)} %embed.1.refs_0_.refs_2_, bf16[1024,512]{1,0:T(8,128)(2,1)S(1)} %collective-permute-done.2.refs_1_.refs_3_, ...), custom_call_target="tpu_custom_call" | custom-call | flops 268435456 | bytes 3670016 | tf_op jit(solution)/shard_map/share_3/pallas_call | solution.py:201
  20.3 1.3 %collective-permute-start.6 = (bf16[128,512]{1,0:T(8,128)(2,1)S(1)}, bf16[128,512]{1,0:T(8,128)(2,1)S(1)}, u32[]{:S(2)}, u32[]{:S(2)}) collective-permute-start(bf16[128,512]{1,0:T(8,128)(2,1)S(1)} %get-tuple-element.62), channel_id=1, source_target_pairs={{0,2},{1,3},{2,0},{3,1},{4,6},{5,7},{6,4},{7,5},{8,10},{9,11},{10,... | collective-permute-start | bytes 393224 | tf_op jit(solution)/shard_map/ppermute | solution.py:289
  21.6 1.5 %share_2.1 = (bf16[128,2048]{1,0:T(8,128)(2,1)S(1)}, bf16[128,2048]{1,0:T(8,128)(2,1)S(1)}, bf16[128,2048]{1,0:T(8,128)(2,1)S(1)}, f32[128,512]{1,0:T(8,128)S(1)...) custom-call(f32[2,2048]{1,0:T(2,128)S(1)} %get-tuple-element.48.refs_0_, ...), custom_call_target="tpu_custom_call" | custom-call | flops 805306368 | bytes 6815744 | tf_op jit(solution)/shard_map/share_2/pallas_call | solution.py:201
  23.1 0.7 %rows_theirs.1 = (bf16[256,512]{1,0:T(8,128)(2,1)S(1)}, bf16[256,512]{1,0:T(8,128)(2,1)S(1)}, bf16[256,512]{1,0:T(8,128)(2,1)S(1)}, bf16[256,512]{1,0:T(8,128)(2,1)S(1)}) custom-call(bf16[128,2048]{1,0:T(8,128)(2,1)S(1)} %get-tuple-element.64.refs_0_, bf16[128,2048]{1,0:T(8,128)(2,1)S(1)} %get-tuple-element.65.refs_1_, ...), custom_call_target="tpu_custom_call" | custom-call | flops 536870912 | bytes 2621440 | tf_op jit(solution)/shard_map/rows_theirs/pallas_call | solution.py:233
  23.8 0.0 copy-start
  23.8 0.1 collective-permute-start.8
  23.9 0.7 %rows_mine.1.refs_0_ = f32[1024,512]{1,0:T(8,128)S(1)} custom-call(bf16[128,2048]{1,0:T(8,128)(2,1)S(1)} %get-tuple-element.64.refs_0_, bf16[128,2048]{1,0:T(8,128)(2,1)S(1)} %get-tuple-element.65.refs_1_, bf16[128,2048]{1,0:T(8,128)(2,1)S(1)} %get-tuple-element.66.refs_2_, bf16[128,2048]{1,0:T(8,128)(2,1)S(1)} %get-tuple-element.67.refs_3_, ...), custom_call_target="tpu_custom_call" | custom-call | flops 536870912 | bytes 2621440 | tf_op jit(solution)/shard_map/rows_mine/pallas_call | solution.py:233
  24.7 0.6 %collective-permute-start.9 = (bf16[256,512]{1,0:T(8,128)(2,1)S(1)}, bf16[256,512]{1,0:T(8,128)(2,1)S(1)}, u32[]{:S(2)}, u32[]{:S(2)}) collective-permute-start(bf16[256,512]{1,0:T(8,128)(2,1)S(1)} %get-tuple-element.70), channel_id=1, source_target_pairs={{0,1},{1,0},{2,3},{3,2},{4,5},{5,4},{6,7},{7,6},{8,9},{9,8},{10,11... | collective-permute-start | bytes 786440 | tf_op jit(solution)/shard_map/ppermute | solution.py:289
  25.2 0.1 collective-permute-start.10
  25.3 0.4 %collective-permute-start.11 = (bf16[256,512]{1,0:T(8,128)(2,1)S(1)}, bf16[256,512]{1,0:T(8,128)(2,1)S(1)}, u32[]{:S(2)}, u32[]{:S(2)}) collective-permute-start(bf16[256,512]{1,0:T(8,128)(2,1)S(1)} %get-tuple-element.72), channel_id=1, source_target_pairs={{0,1},{1,0},{2,3},{3,2},{4,5},{5,4},{6,7},{7,6},{8,9},{9,8},{10,11... | collective-permute-start | bytes 786440 | tf_op jit(solution)/shard_map/ppermute | solution.py:289
  25.7 0.3 collective-permute-done.6
  26.1 2.4 %collective-permute-start.7 = (bf16[128,512]{1,0:T(8,128)(2,1)S(1)}, bf16[128,512]{1,0:T(8,128)(2,1)S(1)}, u32[]{:S(2)}, u32[]{:S(2)}) collective-permute-start(bf16[128,512]{1,0:T(8,128)(2,1)S(1)} %add_convert_fusion), channel_id=1, source_target_pairs={{0,4},{1,5},{2,6},{3,7},{4,0},{5,1},{6,2},{7,3},{8,12},{9,13},{10,... | collective-permute-start | bytes 393224 | tf_op jit(solution)/shard_map/ppermute | solution.py:289
  28.5 1.1 %collective-permute-start.12 = (bf16[128,512]{1,0:T(8,128)(2,1)S(1)}, bf16[128,512]{1,0:T(8,128)(2,1)S(1)}, u32[]{:S(2)}, u32[]{:S(2)}) collective-permute-start(bf16[128,512]{1,0:T(8,128)(2,1)S(1)} %get-tuple-element.75), channel_id=1, source_target_pairs={{0,2},{1,3},{2,0},{3,1},{4,6},{5,7},{6,4},{7,5},{8,10},{9,11},{10,... | collective-permute-start | bytes 393224 | tf_op jit(solution)/shard_map/ppermute | solution.py:289
  29.7 2.1 %back.1 = bf16[1024,1024]{1,0:T(8,128)(2,1)} custom-call(f32[1024,512]{1,0:T(8,128)S(1)} %rows_mine.1.refs_0_, bf16[1024,512]{1,0:T(8,128)(2,1)S(1)} %copy-done, bf16[256,512]{1,0:T(8,128)(2,1)S(1)} %collective-permute-done.8.refs_2_, bf16[256,512]{1,0:T(8,128)(2,1)S(1)} %collective-permute-done.9.refs_3_, ...), custom_call_target="tpu_custom_call" | custom-call | flops 1073741824 | bytes 3145728 | tf_op jit(solution)/shard_map/back/pallas_call | solution.py:265
  31.8 3.3 %collective-permute-done.7 = bf16[128,512]{1,0:T(8,128)(2,1)S(1)} collective-permute-done((bf16[128,512]{1,0:T(8,128)(2,1)S(1)}, bf16[128,512]{1,0:T(8,128)(2,1)S(1)}, u32[]{:S(2)}, u32[]{:S(2)}) %collective-permute-start.7) | collective-permute-done | bytes 131104 | tf_op jit(solution)/shard_map/ppermute | solution.py:289
  35.1 0.8 %collective-permute-done.12 = bf16[128,512]{1,0:T(8,128)(2,1)S(1)} collective-permute-done((bf16[128,512]{1,0:T(8,128)(2,1)S(1)}, bf16[128,512]{1,0:T(8,128)(2,1)S(1)}, u32[]{:S(2)}, u32[]{:S(2)}) %collective-permute-start.12) | collective-permute-done | bytes 131104 | tf_op jit(solution)/shard_map/ppermute | solution.py:289
  35.9 0.8 %add_multiply_fusion = f32[128,512]{1,0:T(8,128)} fusion(bf16[128,512]{1,0:T(8,128)(2,1)S(1)} %collective-permute-done.7, f32[128,512]{1,0:T(8,128)S(1)} %get-tuple-element.74, bf16[128,512]{1,0:T(8,128)(2,1)S(1)} %collective-permute-done.12), kind=kLoop, calls=%fused_computation | loop fusion | flops 327680 | bytes 786432 | tf_op jit(solution)/shard_map/mul | solution.py:339
  (16 shorter events, 0.1 us)
Async XLA Ops:
  0.6 14.6 %copy-start.1 = (bf16[128,512]{1,0:T(8,128)(2,1)S(1)}, bf16[128,512]{1,0:T(8,128)(2,1)}, u32[]{:S(2)}) copy-start(bf16[128,512]{1,0:T(8,128)(2,1)} %refs_4_.5) | copy-start | bytes 393220
  0.6 13.1 %copy-start.4 = (s32[1,64]{1,0:T(1,128)S(1)}, s32[1,64]{1,0:T(1,128)}, u32[]{:S(2)}) copy-start(s32[1,64]{1,0:T(1,128)} %ts_ref.1) | copy-start | bytes 772
  0.7 13.1 %copy-start.3 = (s32[1,64]{1,0:T(1,128)S(1)}, s32[1,64]{1,0:T(1,128)}, u32[]{:S(2)}) copy-start(s32[1,64]{1,0:T(1,128)} %tf_ref.1) | copy-start | bytes 772
  0.7 14.6 %copy-start.2 = (s32[1024]{0:T(1024)S(1)}, s32[1024]{0:T(1024)}, u32[]{:S(2)}) copy-start(s32[1024]{0:T(1024)} %param.10) | copy-start | bytes 12292
  0.7 10.7 %collective-permute-start.1 = (bf16[128,512]{1,0:T(8,128)(2,1)}, bf16[128,512]{1,0:T(8,128)(2,1)S(1)}, u32[]{:S(2)}, u32[]{:S(2)}) collective-permute-start(bf16[128,512]{1,0:T(8,128)(2,1)} %refs_4_.5), channel_id=1, source_target_pairs={{0,4},{1,5},{2,6},{3,7},{4,0},{5,1},{6,2},{7,3},{8,12},{9,13},{10,... | collective-permute-start | bytes 393224 | tf_op jit(solution)/shard_map/ppermute | solution.py:289
  4.8 6.8 %collective-permute-start = (bf16[128,512]{1,0:T(8,128)(2,1)}, bf16[128,512]{1,0:T(8,128)(2,1)S(1)}, u32[]{:S(2)}, u32[]{:S(2)}) collective-permute-start(bf16[128,512]{1,0:T(8,128)(2,1)} %refs_4_.5), channel_id=1, source_target_pairs={{0,2},{1,3},{2,0},{3,1},{4,6},{5,7},{6,4},{7,5},{8,10},{9,11},{10,... | collective-permute-start | bytes 393224 | tf_op jit(solution)/shard_map/ppermute | solution.py:289
  11.6 3.6 %collective-permute-start.2 = (bf16[1024,512]{1,0:T(8,128)(2,1)S(1)}, bf16[1024,512]{1,0:T(8,128)(2,1)S(1)}, u32[]{:S(2)}, u32[]{:S(2)}) collective-permute-start(bf16[1024,512]{1,0:T(8,128)(2,1)S(1)} %embed.1.refs_0_.refs_2_), channel_id=1, source_target_pairs={{0,1},{1,0},{2,3},{3,2},{4,5},{5,4},{6,7},{7,6},{8,9},{9,8},{10,11... | collective-permute-start | bytes 3145736 | tf_op jit(solution)/shard_map/ppermute | solution.py:289
  11.6 6.1 %collective-permute-start.4 = (bf16[128,512]{1,0:T(8,128)(2,1)S(1)}, bf16[128,512]{1,0:T(8,128)(2,1)S(1)}, u32[]{:S(2)}, u32[]{:S(2)}) collective-permute-start(bf16[128,512]{1,0:T(8,128)(2,1)S(1)} %collective-permute-done.1.refs_5_), channel_id=1, source_target_pairs={{0,2},{1,3},{2,0},{3,1},{4,6},{5,7},{6,4},{7,5},{8,10},{9,11},{10,... | collective-permute-start | bytes 393224 | tf_op jit(solution)/shard_map/ppermute | solution.py:289
  14.0 1.2 %collective-permute-start.3 = (f32[4,1024]{1,0:T(4,128)S(1)}, f32[4,1024]{1,0:T(4,128)S(1)}, u32[]{:S(2)}, u32[]{:S(2)}) collective-permute-start(f32[4,1024]{1,0:T(4,128)S(1)} %get-tuple-element.42), channel_id=1, source_target_pairs={{0,1},{1,0},{2,3},{3,2},{4,5},{5,4},{6,7},{7,6},{8,9},{9,8},{10,11... | collective-permute-start | bytes 49160 | tf_op jit(solution)/shard_map/ppermute | solution.py:289
  18.6 1.2 %collective-permute-start.5 = (f32[2,2048]{1,0:T(2,128)S(1)}, f32[2,2048]{1,0:T(2,128)S(1)}, u32[]{:S(2)}, u32[]{:S(2)}) collective-permute-start(f32[2,2048]{1,0:T(2,128)S(1)} %get-tuple-element.48.refs_0_), channel_id=1, source_target_pairs={{0,1},{1,0},{2,3},{3,2},{4,5},{5,4},{6,7},{7,6},{8,9},{9,8},{10,11... | collective-permute-start | bytes 49160 | tf_op jit(solution)/shard_map/ppermute | solution.py:289
  20.3 5.7 %collective-permute-start.6 = (bf16[128,512]{1,0:T(8,128)(2,1)S(1)}, bf16[128,512]{1,0:T(8,128)(2,1)S(1)}, u32[]{:S(2)}, u32[]{:S(2)}) collective-permute-start(bf16[128,512]{1,0:T(8,128)(2,1)S(1)} %get-tuple-element.62), channel_id=1, source_target_pairs={{0,2},{1,3},{2,0},{3,1},{4,6},{5,7},{6,4},{7,5},{8,10},{9,11},{10,... | collective-permute-start | bytes 393224 | tf_op jit(solution)/shard_map/ppermute | solution.py:289
  23.8 5.8 %copy-start = (bf16[1024,512]{1,0:T(8,128)(2,1)S(1)}, bf16[1024,512]{1,0:T(8,128)(2,1)}, u32[]{:S(2)}) copy-start(bf16[1024,512]{1,0:T(8,128)(2,1)} %refs_1_.1) | copy-start | bytes 3145732
  23.8 4.7 %collective-permute-start.8 = (bf16[256,512]{1,0:T(8,128)(2,1)S(1)}, bf16[256,512]{1,0:T(8,128)(2,1)S(1)}, u32[]{:S(2)}, u32[]{:S(2)}) collective-permute-start(bf16[256,512]{1,0:T(8,128)(2,1)S(1)} %get-tuple-element.69), channel_id=1, source_target_pairs={{0,1},{1,0},{2,3},{3,2},{4,5},{5,4},{6,7},{7,6},{8,9},{9,8},{10,11... | collective-permute-start | bytes 786440 | tf_op jit(solution)/shard_map/ppermute | solution.py:289
  24.7 5.0 %collective-permute-start.9 = (bf16[256,512]{1,0:T(8,128)(2,1)S(1)}, bf16[256,512]{1,0:T(8,128)(2,1)S(1)}, u32[]{:S(2)}, u32[]{:S(2)}) collective-permute-start(bf16[256,512]{1,0:T(8,128)(2,1)S(1)} %get-tuple-element.70), channel_id=1, source_target_pairs={{0,1},{1,0},{2,3},{3,2},{4,5},{5,4},{6,7},{7,6},{8,9},{9,8},{10,11... | collective-permute-start | bytes 786440 | tf_op jit(solution)/shard_map/ppermute | solution.py:289
  25.2 4.4 %collective-permute-start.10 = (bf16[256,512]{1,0:T(8,128)(2,1)S(1)}, bf16[256,512]{1,0:T(8,128)(2,1)S(1)}, u32[]{:S(2)}, u32[]{:S(2)}) collective-permute-start(bf16[256,512]{1,0:T(8,128)(2,1)S(1)} %get-tuple-element.71), channel_id=1, source_target_pairs={{0,1},{1,0},{2,3},{3,2},{4,5},{5,4},{6,7},{7,6},{8,9},{9,8},{10,11... | collective-permute-start | bytes 786440 | tf_op jit(solution)/shard_map/ppermute | solution.py:289
  25.3 4.3 %collective-permute-start.11 = (bf16[256,512]{1,0:T(8,128)(2,1)S(1)}, bf16[256,512]{1,0:T(8,128)(2,1)S(1)}, u32[]{:S(2)}, u32[]{:S(2)}) collective-permute-start(bf16[256,512]{1,0:T(8,128)(2,1)S(1)} %get-tuple-element.72), channel_id=1, source_target_pairs={{0,1},{1,0},{2,3},{3,2},{4,5},{5,4},{6,7},{7,6},{8,9},{9,8},{10,11... | collective-permute-start | bytes 786440 | tf_op jit(solution)/shard_map/ppermute | solution.py:289
  26.1 9.0 %collective-permute-start.7 = (bf16[128,512]{1,0:T(8,128)(2,1)S(1)}, bf16[128,512]{1,0:T(8,128)(2,1)S(1)}, u32[]{:S(2)}, u32[]{:S(2)}) collective-permute-start(bf16[128,512]{1,0:T(8,128)(2,1)S(1)} %add_convert_fusion), channel_id=1, source_target_pairs={{0,4},{1,5},{2,6},{3,7},{4,0},{5,1},{6,2},{7,3},{8,12},{9,13},{10,... | collective-permute-start | bytes 393224 | tf_op jit(solution)/shard_map/ppermute | solution.py:289
  28.5 7.4 %collective-permute-start.12 = (bf16[128,512]{1,0:T(8,128)(2,1)S(1)}, bf16[128,512]{1,0:T(8,128)(2,1)S(1)}, u32[]{:S(2)}, u32[]{:S(2)}) collective-permute-start(bf16[128,512]{1,0:T(8,128)(2,1)S(1)} %get-tuple-element.75), channel_id=1, source_target_pairs={{0,2},{1,3},{2,0},{3,1},{4,6},{5,7},{6,4},{7,5},{8,10},{9,11},{10,... | collective-permute-start | bytes 393224 | tf_op jit(solution)/shard_map/ppermute | solution.py:289
